TPU v7x, 512 devices: a whole 4x8x8 slice. The times are simulated.
512 devices in a mesh: rep: 4 (over z_hi), fsdp: 128 (over z_lo, x, y, core).
Axes of the slice: x: 4, y: 8, z: 8 (z_hi: 4, z_lo: 2; z = z_hi * 2 + z_lo), core: 2. Of those that a mesh axis runs over, the one named last changes fastest.
Arguments:
- tokens: bfloat16 [131072, 2304], P(('rep', 'fsdp')), may hold values from -24 to 24
- weight: bfloat16 [4, 2304, 1024], P('rep', 'fsdp'), may hold values from -0.125 to 0.125
- gain: bfloat16 [4, 2304], P('rep', 'fsdp'), may hold values from 0.25 to 1.75
- cotangent: bfloat16 [131072, 1024], P(('rep', 'fsdp')), may hold values from -6 to 6
- outer_delta: bfloat16 [4, 4, 2304, 1024], P('rep', None, 'fsdp'), may hold values from -6 to 6
- global_params: float32 [4, 2304, 1024], P(None, 'fsdp'), may hold values from -6 to 6
- momentum: float32 [4, 2304, 1024], P(None, 'fsdp'), may hold values from -6 to 6
- plan: int32 [4], replicated, may hold values 0 or 1
Outputs:
- layer_out: bfloat16 [131072, 1024], P(('rep', 'fsdp'))
- input_grad: bfloat16 [131072, 2304], P(('rep', 'fsdp'))
- weight_grad: float32 [4, 2304, 1024], P('rep', 'fsdp')
- gain_grad: float32 [4, 2304], P('rep', 'fsdp')
- new_params: float32 [4, 2304, 1024], P(None, 'fsdp')
- new_momentum: float32 [4, 2304, 1024], P(None, 'fsdp')
All inputs are finite; a program needn't handle non-finite values.
Results may differ from a plain program's by a relative error of at most 0.008.
Values may be sent and summed in bfloat16 or wider, within the bound.
No kernel may reach another device: no remote copies, remote signals or barrier semaphores. Data moves between devices by JAX's collectives and lax.ppermute only.
A program may use at most 128 MiB of HBM per device.

v0:
```python
import math

import jax
import jax.numpy as jnp
from jax import lax
from jax.sharding import PartitionSpec as P

epsilon = 1e-06
outer_beta = 0.9
outer_rate = 0.7


def outer_step(average, params, moment, chosen):
    moved = outer_beta * moment + average
    fresh_moment = jnp.where(chosen, moved, moment)
    fresh_params = jnp.where(chosen, params - outer_rate * (average + outer_beta * moved), params)
    return (fresh_params, fresh_moment)


def local(tokens, weight, gain, cotangent, outer_delta, global_params, momentum, plan):
    devices = lax.axis_size("fsdp")
    widened = tokens.astype(jnp.float32)
    recip = lax.rsqrt(jnp.mean(widened * widened, -1, keepdims=True) + epsilon)
    whole_weight, whole_gain = (
        lax.all_gather(weight, "fsdp", axis=1, tiled=True),
        lax.all_gather(gain, "fsdp", axis=1, tiled=True),
    )
    whole_weight = whole_weight[0]
    gain_wide = whole_gain[0].astype(jnp.float32)
    normed = (widened * recip * gain_wide).astype(jnp.bfloat16)
    layer_out = jnp.dot(normed, whole_weight, preferred_element_type=jnp.float32).astype(
        jnp.bfloat16
    )
    normed_grad = jnp.dot(cotangent, whole_weight.T, preferred_element_type=jnp.float32)
    scaled = normed_grad * gain_wide
    inner = jnp.mean(scaled * widened, -1, keepdims=True)
    input_grad = (recip * scaled - widened * recip * recip * recip * inner).astype(jnp.bfloat16)
    width = tokens.shape[1]
    partial_weight = jnp.dot(normed.T, cotangent, preferred_element_type=jnp.float32)
    partial_gain = jnp.sum(normed_grad * widened * recip, 0)
    blocks_weight = partial_weight.reshape(devices, width // devices, partial_weight.shape[1])
    blocks_gain = partial_gain.reshape(devices, width // devices)
    recv_weight, recv_gain = (
        lax.all_to_all(
            blocks_weight.astype(jnp.bfloat16), "fsdp", split_axis=0, concat_axis=0, tiled=True
        ).astype(blocks_weight.dtype),
        lax.all_to_all(
            blocks_gain.astype(jnp.bfloat16), "fsdp", split_axis=0, concat_axis=0, tiled=True
        ).astype(blocks_gain.dtype),
    )
    summed_weight = jnp.sum(recv_weight, 0)
    summed_gain = jnp.sum(recv_gain, 0)
    factor = 1.0 / math.sqrt(tokens.shape[0] * devices)
    weight_grad = (summed_weight * factor)[None]
    gain_grad = (summed_gain * factor)[None]
    replicas = lax.axis_size("rep")
    chosen = (plan == 1)[:, None, None]
    summed = lax.psum(outer_delta[0].astype(jnp.float32).astype(jnp.bfloat16), "rep").astype(
        jnp.float32
    )
    new_params, new_momentum = outer_step(summed / replicas, global_params, momentum, chosen)
    return (layer_out, input_grad, weight_grad, gain_grad, new_params, new_momentum)


def solution(mesh):
    return jax.shard_map(
        local,
        mesh=mesh,
        in_specs=(
            P(("rep", "fsdp"), None),
            P("rep", "fsdp", None),
            P("rep", "fsdp"),
            P(("rep", "fsdp"), None),
            P("rep", None, "fsdp", None),
            P(None, "fsdp", None),
            P(None, "fsdp", None),
            P(),
        ),
        out_specs=(
            P(("rep", "fsdp"), None),
            P(("rep", "fsdp"), None),
            P("rep", "fsdp", None),
            P("rep", "fsdp"),
            P(None, "fsdp", None),
            P(None, "fsdp", None),
        ),
        check_vma=False,
    )
```

profile of v0, /device:TPU:1, one launch (start us, length us, event | category | flops | bytes accessed | tf_op | source)
XLA Modules:
  0.0 489.4 jit_solution(313435695864562220)
XLA Ops:
  8.0 0.0 copy-start
  8.0 0.0 all-reduce.3.cloned.1.call-start
  8.1 0.7 all-reduce.3.cloned.1.call-update
  8.7 0.0 all-gather.2.cloned.1.call-start
  8.8 1.5 copy.16
  10.3 0.0 all-gather.2.cloned.1.call-update
  10.3 1.3 dynamic-slice
  12.2 0.9 dynamic-update-slice
  13.1 286.2 %all-reduce = bf16[2304]{0:T(1024)(128)(2,1)S(1)} all-reduce(bf16[2304]{0:T(1024)(128)(2,1)S(1)} %dynamic-update-slice), channel_id=1, replica_groups=mesh['rep'=4,'fsdp'=128] {'fsdp'}, use_global_device_ids=true, to_apply=%add | all-reduce | flops 2304 | bytes 9216
  299.3 1.6 fusion.11
  300.9 0.0 copy-done
  300.9 4.9 %convolution_convert_fusion = bf16[2304,1024]{1,0:T(8,128)(2,1)} fusion(bf16[256,1024]{1,0:T(8,128)(2,1)S(1)} %copy-done, bf16[256,2304]{1,0:T(8,128)(2,1)} %param.8, f32[2304]{0:T(1024)S(1)} %mul.139, f32[256]{0:T(256)S(1)} %add_rsqrt_fusion), kind=kOutput, calls=%fused_computation.1 | convolution fusion | flops 1212678144 | bytes 6432768 | tf_op jit(solution)/shard_map/dot_general | solution.py:39
  305.8 7.6 %convert_element_type.50 = bf16[128,18,1024]{2,1,0:T(8,128)(2,1)} reshape(bf16[2304,1024]{1,0:T(8,128)(2,1)} %convolution_convert_fusion) | data formatting | bytes 9437184 | tf_op jit(solution)/shard_map/convert_element_type | solution.py:45
  313.4 0.0 copy-start.5
  313.4 0.0 copy-start.3
  313.4 0.0 copy-start.4
  313.4 0.0 copy-start.1
  313.4 8.6 %all-to-all-start = ((bf16[128,18,1024]{2,1,0:T(8,128)(2,1)}), bf16[128,18,1024]{2,1,0:T(8,128)(2,1)}, u32[]{:S(2)}, u32[]{:S(2)}) async-start(bf16[128,18,1024]{2,1,0:T(8,128)(2,1)} %convert_element_type.50), calls=%async_computation | async-start | bytes 12582912 | tf_op jit(solution)/shard_map/all_to_all | solution.py:44
  322.0 0.0 copy-done.5
  322.0 0.0 all-reduce.3.cloned.1.call-done
  322.0 0.0 copy-done.3
  322.0 0.0 copy-done.4
  322.0 2.0 fusion.22
  324.0 0.0 all-gather.2.cloned.1.call-done
  324.0 0.0 copy-done.1
  324.1 7.4 %fusion.14 = (bf16[2304]{0:T(1024)(128)(2,1)S(1)}, f32[256]{0:T(256)S(1)}, f32[256,2304]{1,0:T(8,128)}) fusion(bf16[256,2304]{1,0:T(8,128)(2,1)S(1)} %copy-done.1, f32[256]{0:T(256)S(1)} %add_rsqrt_fusion, f32[2304]{0:T(1024)S(1)} %mul.139, bf16[256,1024]{1,0:T(8,128)(2,1)S(1)} %copy-done, bf16[1,2304,1024]{2,0,1:T(2,128)(2,1)} %all-gather.2.cloned.1.call-done), kind=kOutput, calls=%fused_computation.20 | convolution fusion | flops 1212085760 | bytes 8797696 | tf_op jit(solution)/shard_map/dot_general | solution.py:34
  331.5 0.8 convert_element_type.56
  332.3 0.0 copy-start.2
  332.3 6.3 %fusion.17 = bf16[256,1024]{1,0:T(8,128)(2,1)} fusion(bf16[1,2304,1024]{2,0,1:T(2,128)(2,1)} %all-gather.2.cloned.1.call-done, bf16[256,2304]{1,0:T(8,128)(2,1)S(1)} %copy-done.1, f32[2304]{0:T(1024)S(1)} %mul.139, f32[256]{0:T(256)S(1)} %add_rsqrt_fusion), kind=kOutput, calls=%fused_computation.23 | convolution fusion | flops 1210580992 | bytes 6432768 | tf_op jit(solution)/shard_map/dot_general | solution.py:31
  338.6 0.0 copy-done.2
  338.6 1.8 fusion.10
  340.4 121.6 %all-to-all-done = bf16[128,18,1024]{2,1,0:T(8,128)(2,1)} async-done(((bf16[128,18,1024]{2,1,0:T(8,128)(2,1)}), bf16[128,18,1024]{2,1,0:T(8,128)(2,1)}, u32[]{:S(2)}, u32[]{:S(2)}) %all-to-all-start) | async-done | bytes 4718624 | tf_op jit(solution)/shard_map/all_to_all | solution.py:44
  461.9 8.8 %all-to-all-start.1 = ((bf16[128,1,18]{2,1,0:T(2,128)(2,1)}), bf16[128,1,18]{2,1,0:T(2,128)(2,1)S(1)}, u32[]{:S(2)}, u32[]{:S(2)}) async-start(bf16[128,1,18]{2,1,0:T(2,128)(2,1)} %convert_element_type.56), calls=%async_computation.1 | async-start | bytes 131072 | tf_op jit(solution)/shard_map/all_to_all | solution.py:47
  470.7 4.2 convert_reduce_fusion
  474.9 0.7 mul.129
  475.6 5.7 %all-to-all-done.1 = bf16[128,1,18]{2,1,0:T(2,128)(2,1)S(1)} async-done(((bf16[128,1,18]{2,1,0:T(2,128)(2,1)}), bf16[128,1,18]{2,1,0:T(2,128)(2,1)S(1)}, u32[]{:S(2)}, u32[]{:S(2)}) %all-to-all-start.1) | async-done | bytes 4640 | tf_op jit(solution)/shard_map/all_to_all | solution.py:47
  481.3 0.2 convert_reduce_fusion.1
  481.5 0.5 multiply_bitcast_fusion
  (6 shorter events, 0.0 us)
Async XLA Ops:
  8.0 292.9 %copy-start = (bf16[256,1024]{1,0:T(8,128)(2,1)S(1)}, bf16[256,1024]{1,0:T(8,128)(2,1)}, u32[]{:S(2)}) copy-start(bf16[256,1024]{1,0:T(8,128)(2,1)} %param.11) | copy-start | bytes 1572868
  8.0 314.0 %all-reduce.3.cloned.1.call-start = ((), (), s32[]{:S(2)}) async-start(), calls=%async_computation.3 | async-start | bytes 294912 | tf_op jit(solution)/shard_map/psum | solution.py:58
  8.7 315.3 %all-gather.2.cloned.1.call-start = ((), (), s32[]{:S(2)}) async-start(), calls=%async_computation.2 | async-start | bytes 9510912 | tf_op jit(solution)/shard_map/all_gather | solution.py:25
  313.4 8.6 %copy-start.5 = (s32[4]{0:T(128)S(1)}, s32[4]{0:T(128)}, u32[]{:S(2)}) copy-start(s32[4]{0:T(128)} %param.15) | copy-start | bytes 52
  313.4 8.7 %copy-start.3 = (f32[4,18,1024]{2,0,1:T(4,128)S(1)}, f32[4,18,1024]{2,0,1:T(4,128)}, u32[]{:S(2)}) copy-start(f32[4,18,1024]{2,0,1:T(4,128)} %param.14) | copy-start | bytes 884740
  313.4 8.7 %copy-start.4 = (f32[4,18,1024]{2,0,1:T(4,128)S(1)}, f32[4,18,1024]{2,0,1:T(4,128)}, u32[]{:S(2)}) copy-start(f32[4,18,1024]{2,0,1:T(4,128)} %param.13) | copy-start | bytes 884740
  313.4 10.7 %copy-start.1 = (bf16[256,2304]{1,0:T(8,128)(2,1)S(1)}, bf16[256,2304]{1,0:T(8,128)(2,1)}, u32[]{:S(2)}) copy-start(bf16[256,2304]{1,0:T(8,128)(2,1)} %param.8) | copy-start | bytes 3538948
  313.4 148.6 %all-to-all-start = ((bf16[128,18,1024]{2,1,0:T(8,128)(2,1)}), bf16[128,18,1024]{2,1,0:T(8,128)(2,1)}, u32[]{:S(2)}, u32[]{:S(2)}) async-start(bf16[128,18,1024]{2,1,0:T(8,128)(2,1)} %convert_element_type.50), calls=%async_computation | async-start | bytes 12582912 | tf_op jit(solution)/shard_map/all_to_all | solution.py:44
  332.3 6.3 %copy-start.2 = (f32[256,2304]{1,0:T(8,128)S(1)}, f32[256,2304]{1,0:T(8,128)}, u32[]{:S(2)}) copy-start(f32[256,2304]{1,0:T(8,128)} %get-tuple-element.10) | copy-start | bytes 7077892
  461.9 19.4 %all-to-all-start.1 = ((bf16[128,1,18]{2,1,0:T(2,128)(2,1)}), bf16[128,1,18]{2,1,0:T(2,128)(2,1)S(1)}, u32[]{:S(2)}, u32[]{:S(2)}) async-start(bf16[128,1,18]{2,1,0:T(2,128)(2,1)} %convert_element_type.56), calls=%async_computation.1 | async-start | bytes 131072 | tf_op jit(solution)/shard_map/all_to_all | solution.py:47
Sparse Core Ops, SparseCore 0:
  11.8 59.9 all-reduce.2
Sparse Core Ops, SparseCore 1:
  12.0 230.2 all-gather.1
where the time goes:
time: 490 us; the launch traced here: 489 us
  blocking collectives  286 us (58%)
  waiting for transfers between devices  128 us (26%)
  matrix products  18.6 us (4%)
  starting transfers between devices  17.4 us (4%)
  between operations  16.2 us (3%)
  local copies, waits for them, and re-layouts  12.7 us (3%)
  other arithmetic  10.3 us (2%)
    unnamed x1, blocking collectives  286 us
    all_to_all x1, waiting for transfers between devices, local(): lax.all_to_all(blocks_weight.astype(jnp.bfloat16), 'fsdp', split_axis=0,...  122 us
  transfers between devices with their start and end apart: 4, of which 2 were waited for; matrix products, arithmetic and copies ran while one was open for 8% of the time, Pallas kernels for 0%

commit v1 on v0

v1 whole, which is shorter than its diff:
```python
import functools
import math

import jax
import jax.numpy as jnp
from jax import lax
from jax.experimental import pallas as pl
from jax.experimental.pallas import tpu as pltpu
from jax.sharding import Mesh
from jax.sharding import PartitionSpec as P

epsilon = 1e-06
outer_beta = 0.9
outer_rate = 0.7
FSDP = ("z", "x", "y", "core")
ALL = ("rep",) + FSDP
f32, bf16 = jnp.float32, jnp.bfloat16


def outer_step(average, params, moment, chosen):
    moved = outer_beta * moment + average
    fresh_moment = jnp.where(chosen, moved, moment)
    fresh_params = jnp.where(chosen, params - outer_rate * (average + outer_beta * moved), params)
    return (fresh_params, fresh_moment)


def swap(values):
    return lax.ppermute(values, "core", [(0, 1), (1, 0)])


def exchange(values, axes):
    return lax.all_to_all(values, axes, split_axis=0, concat_axis=0, tiled=True)


def vmem(shape, index=None):
    return pl.BlockSpec(shape, index or (lambda *_: (0,) * len(shape)))


def params(mebibytes=40):
    return pltpu.CompilerParams(vmem_limit_bytes=mebibytes * 2**20)


def cost(flops, moved):
    return pl.CostEstimate(flops=flops, bytes_accessed=moved, transcendentals=0)


def row_recip(wide):
    return lax.rsqrt(jnp.mean(wide * wide, -1, keepdims=True) + epsilon)


def shrink_kernel(core_ref, tokens_ref, cot_ref, mine_ref, theirs_ref):
    half = mine_ref.shape[1]
    recip = row_recip(tokens_ref[...].astype(f32))
    here = pl.multiple_of(core_ref[0] * half, half)
    there = pl.multiple_of((1 - core_ref[0]) * half, half)
    mine_ref[...] = (cot_ref[:, pl.ds(here, half)].astype(f32) * recip).astype(bf16)
    theirs_ref[...] = (cot_ref[:, pl.ds(there, half)].astype(f32) * recip).astype(bf16)


def shrink(core, tokens, cotangent):
    rows, out = cotangent.shape
    half = jax.ShapeDtypeStruct((rows, out // 2), bf16)
    return pl.pallas_call(
        shrink_kernel,
        out_shape=(half, half),
        in_specs=[
            pl.BlockSpec(memory_space=pltpu.SMEM),
            pl.BlockSpec(memory_space=pltpu.VMEM),
            pl.BlockSpec(memory_space=pltpu.VMEM),
        ],
        out_specs=(pl.BlockSpec(memory_space=pltpu.VMEM),) * 2,
        compiler_params=params(),
        cost_estimate=cost(4 * tokens.size, 2 * tokens.size + 4 * cotangent.size),
        name="shrink",
    )(core, tokens, cotangent)


def partial_kernel(tokens_ref, others_ref, mine_ref, theirs_ref, out_ref):
    over_rows = (((0,), (0,)), ((), ()))
    first = lax.dot_general(
        tokens_ref[...], mine_ref[...], over_rows, preferred_element_type=f32
    )
    second = lax.dot_general(
        others_ref[...], theirs_ref[...], over_rows, preferred_element_type=f32
    )
    out_ref[...] = (first + second).astype(bf16)


def partial_product(tokens, others, mine, theirs):
    rows, width = tokens.shape
    half = mine.shape[1]
    step = width // 6
    return pl.pallas_call(
        partial_kernel,
        grid=(6,),
        out_shape=jax.ShapeDtypeStruct((width, half), bf16),
        in_specs=[
            pl.BlockSpec((rows, step), lambda i: (0, i)),
            pl.BlockSpec((rows, step), lambda i: (0, i)),
            vmem((rows, half)),
            vmem((rows, half)),
        ],
        out_specs=pl.BlockSpec((step, half), lambda i: (i, 0)),
        compiler_params=params(),
        cost_estimate=cost(4 * rows * width * half, 6 * rows * width),
        name="partial",
    )(tokens, others, mine, theirs)


def plane_kernel(parts_ref, out_ref):
    total = parts_ref[0].astype(f32)
    for i in range(1, parts_ref.shape[0]):
        total = total + parts_ref[i].astype(f32)
    own = out_ref.shape[1]
    for i in range(out_ref.shape[0]):
        out_ref[i] = total[i * own : (i + 1) * own].astype(bf16)


def plane_total(parts, owners):
    planes, rows, half = parts.shape
    return pl.pallas_call(
        plane_kernel,
        out_shape=jax.ShapeDtypeStruct((owners, rows // owners, half), bf16),
        compiler_params=params(),
        cost_estimate=cost(parts.size, 3 * parts.size),
        name="plane_total",
    )(parts)


def owner_kernel(factor, blocks_ref, weight_ref, gain_ref, weight_grad_ref, gain_grad_ref):
    half = blocks_ref.shape[2]
    dots = 0.0
    for core in range(2):
        total = blocks_ref[core].astype(f32)
        for column in range(1, blocks_ref.shape[0] // 2):
            total = total + blocks_ref[2 * column + core].astype(f32)
        total = total * factor
        columns = slice(core * half, (core + 1) * half)
        weight_grad_ref[0, :, columns] = total * gain_ref[...].astype(f32)
        dots = dots + jnp.sum(total * weight_ref[0, :, columns].astype(f32), -1, keepdims=True)
    gain_grad_ref[...] = dots


def owner_total(factor, blocks, weight, gain):
    own = weight.shape[1]
    return pl.pallas_call(
        functools.partial(owner_kernel, factor),
        out_shape=(
            jax.ShapeDtypeStruct(weight.shape, f32),
            jax.ShapeDtypeStruct((own, 1), f32),
        ),
        compiler_params=params(),
        cost_estimate=cost(blocks.size, 3 * blocks.size),
        name="owner_total",
    )(blocks, weight, gain)


def project_kernel(
    core_ref, tokens_ref, cot_ref, mine_ref, theirs_ref,
    layer_ref, grad_ref, whole, product, scaled,
):
    step = pl.program_id(0)
    columns, rows, half = mine_ref.shape
    band = whole.shape[0]
    group = 36
    for side, ref in enumerate((mine_ref, theirs_ref)):
        side_core = core_ref[0] if side == 0 else 1 - core_ref[0]
        place = pl.multiple_of(side_core * half, half)
        for plane in range(rows // group):
            piece = jnp.concatenate(
                [ref[y, plane * group : (plane + 1) * group, :] for y in range(columns)], 0
            )
            block = columns * group
            whole[plane * block : (plane + 1) * block, pl.ds(place, half)] = piece
    start = pl.multiple_of(step * band, 128)
    contribution = jnp.dot(
        tokens_ref[:, pl.ds(start, band)], whole[...], preferred_element_type=f32
    )
    scaled[step] = lax.dot_general(
        cot_ref[...], whole[...], (((1,), (1,)), ((), ())), preferred_element_type=f32
    )

    @pl.when(step == 0)
    def _():
        product[...] = contribution

    @pl.when(step == pl.num_programs(0) - 1)
    def _():
        width = tokens_ref.shape[1]
        wide = tokens_ref[...].astype(f32)
        recip = row_recip(wide)
        full = product[...] + contribution
        layer_ref[...] = (full * recip).astype(bf16)
        inner = jnp.sum(full * cot_ref[...].astype(f32), -1, keepdims=True) / width
        slope = recip * recip * recip * inner
        for part in range(2):
            lanes = slice(part * band, (part + 1) * band)
            grad = recip * scaled[part] - tokens_ref[:, lanes].astype(f32) * slope
            grad_ref[:, lanes] = grad.astype(bf16)


def project(core, tokens, cotangent, mine, theirs):
    rows, width = tokens.shape
    out = cotangent.shape[1]
    columns, per, half = mine.shape
    band = width // 2
    return pl.pallas_call(
        project_kernel,
        grid=(2,),
        out_shape=(
            jax.ShapeDtypeStruct((rows, out), bf16),
            jax.ShapeDtypeStruct((rows, width), bf16),
        ),
        in_specs=[
            pl.BlockSpec(memory_space=pltpu.SMEM),
            vmem((rows, width)),
            vmem((rows, out)),
            pl.BlockSpec((columns, per // 2, half), lambda i: (0, i, 0)),
            pl.BlockSpec((columns, per // 2, half), lambda i: (0, i, 0)),
        ],
        out_specs=(vmem((rows, out)), vmem((rows, width))),
        scratch_shapes=[
            pltpu.VMEM((band, out), bf16),
            pltpu.VMEM((rows, out), f32),
            pltpu.VMEM((2, rows, band), f32),
        ],
        compiler_params=params(48),
        cost_estimate=cost(4 * rows * width * out, 2 * width * out + 4 * rows * (width + out)),
        name="project",
    )(core, tokens, cotangent, mine, theirs)


def local(tokens, weight, gain, cotangent, outer_delta, global_params, momentum, plan):
    out = weight.shape[2]
    own, half = weight.shape[1], out // 2
    planes = lax.axis_size("z") * lax.axis_size("x")
    columns = lax.axis_size("y")
    core = lax.axis_index("core").astype(jnp.int32).reshape(1)
    replicas = lax.axis_size("rep")
    factor = 1.0 / math.sqrt(tokens.shape[0] * planes * columns * 2)

    summed = lax.psum(outer_delta[0], "rep")

    gain_column = gain.reshape(own, 1)
    scaled_weight = (weight[0].astype(f32) * gain_column.astype(f32)).astype(bf16)
    halves = jnp.stack([scaled_weight[:, :half], scaled_weight[:, half:]])
    spread = jnp.broadcast_to(halves[None], (planes, 2, own, half)).reshape(planes * 2, own, half)
    plane = exchange(spread, ("z", "x", "core")).reshape(planes * 2 * own, half)
    gathered = lax.all_gather(plane, "y", axis=0, tiled=True)

    others = swap(tokens)
    mine, theirs = shrink(core, tokens, cotangent)
    partial = partial_product(tokens, others, mine, swap(theirs))
    received = exchange(partial.reshape(planes, columns * 2 * own, half), ("z", "x"))
    plane_sum = plane_total(received, columns * 2)
    plane_sum, gathered, summed = lax.optimization_barrier((plane_sum, gathered, summed))
    blocks = exchange(plane_sum, ("y", "core"))
    weight_grad, gain_grad = owner_total(factor, blocks, weight, gain_column)

    gathered = gathered.reshape(columns, planes * 2 * own, half)
    layer_out, input_grad = project(core, tokens, cotangent, gathered, swap(gathered))

    chosen = (plan == 1)[:, None, None]
    new_params, new_momentum = outer_step(
        summed.astype(f32) / replicas, global_params, momentum, chosen
    )
    return (
        layer_out, input_grad, weight_grad, gain_grad.reshape(1, own), new_params, new_momentum
    )


def solution(mesh):
    fine = Mesh(mesh.devices.reshape(4, 2, 4, 8, 2), ALL)
    return jax.shard_map(
        local,
        mesh=fine,
        in_specs=(
            P(ALL, None),
            P("rep", FSDP, None),
            P("rep", FSDP),
            P(ALL, None),
            P("rep", None, FSDP, None),
            P(None, FSDP, None),
            P(None, FSDP, None),
            P(),
        ),
        out_specs=(
            P(ALL, None),
            P(ALL, None),
            P("rep", FSDP, None),
            P("rep", FSDP),
            P(None, FSDP, None),
            P(None, FSDP, None),
        ),
        check_vma=False,
    )
```

time: 490 us -> 129 us (0.26)
  blocking collectives: 286 us -> 0 us
  waiting for transfers between devices: 128 us -> 55.9 us
  matrix products: 18.6 us -> 0 us
  starting transfers between devices: 17.4 us -> 30.3 us
  Pallas kernels: 0 us -> 11.8 us
  other arithmetic: 10.3 us -> 4.4 us
    unnamed x1 -> x0, blocking collectives: 286 us -> none
    all_to_all x2 -> x3, waiting for transfers between devices: 127 us -> 40.2 us  [exchange(): return lax.all_to_all(values, axes, split_axis=0, concat_axis=0, tiled=True)]
    dot_general x3 -> x0, matrix products: 18.6 us -> none  [the longest x1 7.44 us: local(): jnp.dot(cotangent, whole_weight.T, preferred_element_type=jnp.float32)]
    ppermute x0 -> x3, starting transfers between devices: none -> 17.4 us  [swap(): return lax.ppermute(values, 'core', [(0, 1), (1, 0)])]
    psum x1, waiting for transfers between devices: 0.02 us -> 13.7 us  [local(): summed = lax.psum(outer_delta[0], 'rep')]
    pallas_call x0 -> x5, Pallas kernels: none -> 11.8 us  [the longest x1 6.98 us: project(): pl.pallas_call(project_kernel, grid=(2,), out_shape=(jax.ShapeDtypeStruct...]
    convert_element_type x2 -> x0, local copies, waits for them, and re-layouts: 8.34 us -> none  [the longest x1 7.57 us: local(): blocks_weight.astype(jnp.bfloat16)]
    reduce_sum x3 -> x0, other arithmetic: 5.95 us -> none  [the longest x1 4.22 us: local(): summed_weight = jnp.sum(recv_weight, 0)]
  transfers between devices with their start and end apart: 4 -> 8, of which waited for: 2 -> 5; matrix products, arithmetic and copies ran while one was open for 8% -> 6% of each run, Pallas kernels for 0% -> 4%
where the time goes in v1:
time: 129 us; the launch traced here: 128 us
  waiting for transfers between devices  55.9 us (43%)
  starting transfers between devices  30.3 us (23%)
  between operations  15.6 us (12%)
  Pallas kernels  11.8 us (9%)
  local copies, waits for them, and re-layouts  9.69 us (8%)
  other arithmetic  4.4 us (3%)
    all_to_all x3, waiting for transfers between devices, exchange(): return lax.all_to_all(values, axes, split_axis=0, concat_axis=0, tiled=True)  40.2 us
    ppermute x3, starting transfers between devices, swap(): return lax.ppermute(values, 'core', [(0, 1), (1, 0)])  17.4 us
    psum x1, waiting for transfers between devices, local(): summed = lax.psum(outer_delta[0], 'rep')  13.7 us
    all_to_all x3, starting transfers between devices, exchange(): return lax.all_to_all(values, axes, split_axis=0, concat_axis=0, tiled=True)  12.9 us
    unnamed x21, local copies, waits for them, and re-layouts  6.99 us
    pallas_call x1, Pallas kernels, project(): pl.pallas_call(project_kernel, grid=(2,), out_shape=(jax.ShapeDtypeStruct...  6.98 us
    pallas_call x1, Pallas kernels, partial_product(): pl.pallas_call(partial_kernel, grid=(6,), out_shape=jax.ShapeDtypeStruct(...  4.06 us
  transfers between devices with their start and end apart: 8, of which 5 were waited for; matrix products, arithmetic and copies ran while one was open for 6% of the time, Pallas kernels for 4%

profile of v1, /device:TPU:1, one launch (start us, length us, event | category | flops | bytes accessed | tf_op | source)
XLA Modules:
  0.0 127.8 jit_solution(4217496793145193029)
XLA Ops:
  8.0 0.0 copy-start.1
  8.0 8.9 %collective-permute-start = (bf16[256,2304]{1,0:T(8,128)(2,1)}, bf16[256,2304]{1,0:T(8,128)(2,1)S(1)}, u32[]{:S(2)}, u32[]{:S(2)}) collective-permute-start(bf16[256,2304]{1,0:T(8,128)(2,1)} %tokens_ref.5), channel_id=1, source_target_pairs={{0,1},{1,0},{2,3},{3,2},{4,5},{5,4},{6,7},{7,6},{8,9},{9,8},{10,11... | collective-permute-start | bytes 3538952 | tf_op jit(solution)/shard_map/ppermute | solution.py:28
  16.9 0.7 bitcast_convert_fusion
  17.6 0.9 fusion.1
  18.5 0.8 broadcast_in_dim.18
  19.3 3.5 %all-to-all-start.1 = ((bf16[16,18,512]{2,1,0:T(8,128)(2,1)}), bf16[16,18,512]{2,1,0:T(8,128)(2,1)S(1)}, u32[]{:S(2)}, u32[]{:S(2)}) async-start(bf16[16,18,512]{2,1,0:T(8,128)(2,1)} %bitcast.6), calls=%async_computation.1 | async-start | bytes 786432 | tf_op jit(solution)/shard_map/all_to_all | solution.py:32
  22.7 0.0 all-reduce.2.cloned.1.call-start
  22.8 0.0 copy-start
  22.8 1.3 copy-done
  24.1 0.0 copy-start.3
  24.1 1.0 copy-done.3
  25.1 0.3 shrink.1
  25.4 2.0 %collective-permute-start.1 = (bf16[256,512]{1,0:T(8,128)(2,1)S(1)}, bf16[256,512]{1,0:T(8,128)(2,1)S(1)}, u32[]{:S(2)}, u32[]{:S(2)}) collective-permute-start(bf16[256,512]{1,0:T(8,128)(2,1)S(1)} %get-tuple-element.16), channel_id=1, source_target_pairs={{0,1},{1,0},{2,3},{3,2},{4,5},{5,4},{6,7},{7,6},{8,9},{9,8},{10,11... | collective-permute-start | bytes 786440 | tf_op jit(solution)/shard_map/ppermute | solution.py:28
  27.5 0.0 all-reduce.2.cloned.1.call-update
  27.5 1.4 %collective-permute-done.1.theirs_ref = bf16[256,512]{1,0:T(8,128)(2,1)S(1)} collective-permute-done((bf16[256,512]{1,0:T(8,128)(2,1)S(1)}, bf16[256,512]{1,0:T(8,128)(2,1)S(1)}, u32[]{:S(2)}, u32[]{:S(2)}) %collective-permute-start.1) | collective-permute-done | bytes 262176 | tf_op jit(solution)/shard_map/ppermute | solution.py:28
  28.9 0.0 collective-permute-done.others_ref
  28.9 0.0 copy-done.1
  28.9 4.1 %partial.1 = bf16[2304,512]{1,0:T(8,128)(2,1)} custom-call(bf16[256,2304]{1,0:T(8,128)(2,1)S(1)} %copy-done.1, bf16[256,2304]{1,0:T(8,128)(2,1)S(1)} %collective-permute-done.others_ref, bf16[256,512]{1,0:T(8,128)(2,1)S(1)} %get-tuple-element.15.mine_ref, bf16[256,512]{1,0:T(8,128)(2,1)S(1)} %collective-permute-done.1.theirs_ref), custom_call_target="tpu_custom_call" | custom-call | flops 1207959552 | bytes 3538944 | tf_op jit(solution)/shard_map/partial/pallas_call | solution.py:93
  32.9 0.0 all-to-all-done.1
  32.9 0.0 copy-start.7
  32.9 0.7 copy-done.7
  33.7 5.0 %all-to-all-start = ((bf16[8,288,512]{2,1,0:T(8,128)(2,1)}), bf16[8,288,512]{2,1,0:T(8,128)(2,1)S(1)}, u32[]{:S(2)}, u32[]{:S(2)}) async-start(bf16[8,288,512]{2,1,0:T(8,128)(2,1)} %bitcast.1), calls=%async_computation | async-start | bytes 4718592 | tf_op jit(solution)/shard_map/all_to_all | solution.py:32
  38.7 0.0 copy-start.8
  38.7 0.0 copy-start.9
  38.7 0.0 all-gather.2.cloned.1.call-start
  38.8 1.8 %reshape.49 = bf16[288,512]{1,0:T(8,128)(2,1)} reshape(bf16[16,18,512]{2,1,0:T(8,128)(2,1)} %copy-done.7) | data formatting | bytes 589824 | tf_op jit(solution)/shard_map/reshape | solution.py:248
  40.6 0.0 all-gather.2.cloned.1.call-update
  40.6 28.0 %all-to-all-done.parts_ref = bf16[8,288,512]{2,1,0:T(8,128)(2,1)S(1)} async-done(((bf16[8,288,512]{2,1,0:T(8,128)(2,1)}), bf16[8,288,512]{2,1,0:T(8,128)(2,1)S(1)}, u32[]{:S(2)}, u32[]{:S(2)}) %all-to-all-start) | async-done | bytes 2359328 | tf_op jit(solution)/shard_map/all_to_all | solution.py:32
  68.6 0.3 plane_total.1
  69.0 0.0 copy-start.2
  69.0 0.7 copy-done.2
  69.7 0.0 copy-start.4
  69.7 13.7 %all-reduce.2.cloned.1.call-done = bf16[4,18,1024]{2,0,1:T(4,128)(2,1)} async-done(((bf16[4,18,1024]{2,0,1:T(4,128)(2,1)}), bf16[4,18,1024]{2,0,1:T(4,128)(2,1)}) %all-reduce.2.cloned.1.call-update) | async-done | bytes 147472 | tf_op jit(solution)/shard_map/psum | solution.py:242
  83.5 0.5 all-gather.2.cloned.1.call-done
  84.0 6.4 %collective-permute-start.2 = (bf16[8,288,512]{2,1,0:T(8,128)(2,1)}, bf16[8,288,512]{2,1,0:T(8,128)(2,1)}, u32[]{:S(2)}, u32[]{:S(2)}) collective-permute-start(bf16[8,288,512]{2,1,0:T(8,128)(2,1)} %bitcast.17), channel_id=1, source_target_pairs={{0,1},{1,0},{2,3},{3,2},{4,5},{5,4},{6,7},{7,6},{8,9},{9,8},{10,11... | collective-permute-start | bytes 7077896 | tf_op jit(solution)/shard_map/ppermute | solution.py:28
  90.4 4.4 %all-to-all-start.2 = ((bf16[16,18,512]{2,1,0:T(8,128)(2,1)}), bf16[16,18,512]{2,1,0:T(8,128)(2,1)S(1)}, u32[]{:S(2)}, u32[]{:S(2)}) async-start(bf16[16,18,512]{2,1,0:T(8,128)(2,1)} %copy-done.2), calls=%async_computation.2 | async-start | bytes 786432 | tf_op jit(solution)/shard_map/all_to_all | solution.py:32
  94.8 0.0 copy-done.8
  94.8 0.1 copy.16.gain_ref
  95.0 0.0 copy-done.9
  95.0 2.2 %fusion = (f32[4,18,1024]{2,0,1:T(4,128)}, f32[4,18,1024]{2,0,1:T(4,128)}) fusion(f32[4,18,1024]{2,0,1:T(4,128)} %param.14, bf16[4,18,1024]{2,0,1:T(4,128)(2,1)} %all-reduce.2.cloned.1.call-done, pred[4]{0:T(512)(128)(4,1)S(1)} %broadcast_compare_fusion, f32[4,18,1024]{2,0,1:T(4,128)} %param.13), kind=kLoop, calls=%fused_computation.2 | loop fusion | flops 737280 | bytes 1327108 | tf_op jit(solution)/shard_map/jit(_where)/select_n | solution.py:22
  97.2 12.2 %all-to-all-done.2.blocks_ref = bf16[16,18,512]{2,1,0:T(8,128)(2,1)S(1)} async-done(((bf16[16,18,512]{2,1,0:T(8,128)(2,1)}), bf16[16,18,512]{2,1,0:T(8,128)(2,1)S(1)}, u32[]{:S(2)}, u32[]{:S(2)}) %all-to-all-start.2) | async-done | bytes 294944 | tf_op jit(solution)/shard_map/all_to_all | solution.py:32
  109.4 0.0 copy-start.5
  109.4 0.8 copy-done.5
  110.2 0.1 owner_total.1
  110.3 0.7 copy.17
  111.1 0.6 reduce
  111.7 0.0 collective-permute-done.2.theirs_ref
  111.7 0.0 copy-done.4
  111.7 0.0 copy-start.6
  111.7 1.7 %copy-done.6 = bf16[2304,512]{1,0:T(8,128)(2,1)S(1)} copy-done((bf16[2304,512]{1,0:T(8,128)(2,1)S(1)}, bf16[2304,512]{1,0:T(8,128)(2,1)}, u32[]{:S(2)}) %copy-start.6) | copy-done | bytes 2359320
  113.4 7.0 %project.1 = (bf16[256,1024]{1,0:T(8,128)(2,1)}, bf16[256,2304]{1,0:T(8,128)(2,1)}) custom-call(s32[1]{0:T(128)} %bitcast.core_ref, bf16[256,2304]{1,0:T(8,128)(2,1)S(1)} %copy-done.1, bf16[256,1024]{1,0:T(8,128)(2,1)S(1)} %copy-done.4, bf16[8,288,512]{2,1,0:T(8,128)(2,1)S(1)} %bitcast.18, bf16[8,288,512]{2,1,0:T(8,128)(2,1)} %collective-permute-done.2.theirs_ref), custom_call_target="tpu_custom_call" | custom-call | flops 2415919104 | bytes 8126464 | tf_op jit(solution)/shard_map/project/pallas_call | solution.py:207
  (3 shorter events, 0.0 us)
Async XLA Ops:
  8.0 20.9 %copy-start.1 = (bf16[256,2304]{1,0:T(8,128)(2,1)S(1)}, bf16[256,2304]{1,0:T(8,128)(2,1)}, u32[]{:S(2)}) copy-start(bf16[256,2304]{1,0:T(8,128)(2,1)} %tokens_ref.5) | copy-start | bytes 3538948
  8.0 20.9 %collective-permute-start = (bf16[256,2304]{1,0:T(8,128)(2,1)}, bf16[256,2304]{1,0:T(8,128)(2,1)S(1)}, u32[]{:S(2)}, u32[]{:S(2)}) collective-permute-start(bf16[256,2304]{1,0:T(8,128)(2,1)} %tokens_ref.5), channel_id=1, source_target_pairs={{0,1},{1,0},{2,3},{3,2},{4,5},{5,4},{6,7},{7,6},{8,9},{9,8},{10,11... | collective-permute-start | bytes 3538952 | tf_op jit(solution)/shard_map/ppermute | solution.py:28
  19.3 13.7 %all-to-all-start.1 = ((bf16[16,18,512]{2,1,0:T(8,128)(2,1)}), bf16[16,18,512]{2,1,0:T(8,128)(2,1)S(1)}, u32[]{:S(2)}, u32[]{:S(2)}) async-start(bf16[16,18,512]{2,1,0:T(8,128)(2,1)} %bitcast.6), calls=%async_computation.1 | async-start | bytes 786432 | tf_op jit(solution)/shard_map/all_to_all | solution.py:32
  22.7 60.7 %all-reduce.2.cloned.1.call-start = ((), (), s32[]{:S(2)}) async-start(), calls=%async_computation.4 | async-start | bytes 294912 | tf_op jit(solution)/shard_map/psum | solution.py:242
  22.8 1.3 copy-start
  24.1 1.0 copy-start.3
  25.4 3.4 %collective-permute-start.1 = (bf16[256,512]{1,0:T(8,128)(2,1)S(1)}, bf16[256,512]{1,0:T(8,128)(2,1)S(1)}, u32[]{:S(2)}, u32[]{:S(2)}) collective-permute-start(bf16[256,512]{1,0:T(8,128)(2,1)S(1)} %get-tuple-element.16), channel_id=1, source_target_pairs={{0,1},{1,0},{2,3},{3,2},{4,5},{5,4},{6,7},{7,6},{8,9},{9,8},{10,11... | collective-permute-start | bytes 786440 | tf_op jit(solution)/shard_map/ppermute | solution.py:28
  32.9 0.7 copy-start.7
  33.7 34.9 %all-to-all-start = ((bf16[8,288,512]{2,1,0:T(8,128)(2,1)}), bf16[8,288,512]{2,1,0:T(8,128)(2,1)S(1)}, u32[]{:S(2)}, u32[]{:S(2)}) async-start(bf16[8,288,512]{2,1,0:T(8,128)(2,1)} %bitcast.1), calls=%async_computation | async-start | bytes 4718592 | tf_op jit(solution)/shard_map/all_to_all | solution.py:32
  38.7 56.1 %copy-start.8 = (bf16[1,18]{1,0:T(2,128)(2,1)S(1)}, bf16[1,18]{1,0:T(2,128)(2,1)}, u32[]{:S(2)}) copy-start(bf16[1,18]{1,0:T(2,128)(2,1)} %param.10) | copy-start | bytes 112
  38.7 56.2 %copy-start.9 = (s32[4]{0:T(128)S(1)}, s32[4]{0:T(128)}, u32[]{:S(2)}) copy-start(s32[4]{0:T(128)} %param.15) | copy-start | bytes 52
  38.7 45.3 %all-gather.2.cloned.1.call-start = ((), (), s32[]{:S(2)}) async-start(), calls=%async_computation.3 | async-start | bytes 2654208 | tf_op jit(solution)/shard_map/all_gather | solution.py:249
  69.0 0.7 copy-start.2
  69.7 42.0 %copy-start.4 = (bf16[256,1024]{1,0:T(8,128)(2,1)S(1)}, bf16[256,1024]{1,0:T(8,128)(2,1)}, u32[]{:S(2)}) copy-start(bf16[256,1024]{1,0:T(8,128)(2,1)} %cot_ref.3) | copy-start | bytes 1572868
  84.0 27.7 %collective-permute-start.2 = (bf16[8,288,512]{2,1,0:T(8,128)(2,1)}, bf16[8,288,512]{2,1,0:T(8,128)(2,1)}, u32[]{:S(2)}, u32[]{:S(2)}) collective-permute-start(bf16[8,288,512]{2,1,0:T(8,128)(2,1)} %bitcast.17), channel_id=1, source_target_pairs={{0,1},{1,0},{2,3},{3,2},{4,5},{5,4},{6,7},{7,6},{8,9},{9,8},{10,11... | collective-permute-start | bytes 7077896 | tf_op jit(solution)/shard_map/ppermute | solution.py:28
  90.4 19.0 %all-to-all-start.2 = ((bf16[16,18,512]{2,1,0:T(8,128)(2,1)}), bf16[16,18,512]{2,1,0:T(8,128)(2,1)S(1)}, u32[]{:S(2)}, u32[]{:S(2)}) async-start(bf16[16,18,512]{2,1,0:T(8,128)(2,1)} %copy-done.2), calls=%async_computation.2 | async-start | bytes 786432 | tf_op jit(solution)/shard_map/all_to_all | solution.py:32
  109.4 0.8 copy-start.5
  111.7 1.7 %copy-start.6 = (bf16[2304,512]{1,0:T(8,128)(2,1)S(1)}, bf16[2304,512]{1,0:T(8,128)(2,1)}, u32[]{:S(2)}) copy-start(bf16[2304,512]{1,0:T(8,128)(2,1)} %all-gather.2.cloned.1.call-done) | copy-start | bytes 7077892
Sparse Core Ops, SparseCore 0:
  27.6 55.8 all-reduce.1
Sparse Core Ops, SparseCore 1:
  41.9 42.1 all-gather.1

commit v2 on v1

v2 whole, which is shorter than its diff:
```python
import functools
import math

import jax
import jax.numpy as jnp
from jax import lax
from jax.experimental import pallas as pl
from jax.experimental.pallas import tpu as pltpu
from jax.sharding import Mesh
from jax.sharding import PartitionSpec as P

epsilon = 1e-06
outer_beta = 0.9
outer_rate = 0.7
FSDP = ("z", "x", "y", "core")
ALL = ("rep",) + FSDP
f32, bf16 = jnp.float32, jnp.bfloat16


def outer_step(average, params, moment, chosen):
    moved = outer_beta * moment + average
    fresh_moment = jnp.where(chosen, moved, moment)
    fresh_params = jnp.where(chosen, params - outer_rate * (average + outer_beta * moved), params)
    return (fresh_params, fresh_moment)


def swap(values):
    return lax.ppermute(values, "core", [(0, 1), (1, 0)])


def turn(values, by):
    count = lax.axis_size("y")
    return lax.ppermute(values, "y", [(i, (i + by) % count) for i in range(count)])


def cycle(values, by):
    count = lax.axis_size("rep")
    return lax.ppermute(values, "rep", [(i, (i + by) % count) for i in range(count)])


def exchange(values, axes):
    return lax.all_to_all(values, axes, split_axis=0, concat_axis=0, tiled=True)


def vmem(shape, index=None):
    return pl.BlockSpec(shape, index or (lambda *_: (0,) * len(shape)))


def params(mebibytes=40):
    return pltpu.CompilerParams(vmem_limit_bytes=mebibytes * 2**20)


def cost(flops, moved):
    return pl.CostEstimate(flops=flops, bytes_accessed=moved, transcendentals=0)


def row_recip(wide):
    return lax.rsqrt(jnp.mean(wide * wide, -1, keepdims=True) + epsilon)


def column_of(row):
    count = row.shape[1]
    shape = (count, count)
    same = lax.broadcasted_iota(jnp.int32, shape, 0) == lax.broadcasted_iota(jnp.int32, shape, 1)
    return jnp.sum(jnp.where(same, row, 0.0), 1, keepdims=True)


def row_of(column):
    count = column.shape[0]
    shape = (count, count)
    same = lax.broadcasted_iota(jnp.int32, shape, 0) == lax.broadcasted_iota(jnp.int32, shape, 1)
    return jnp.sum(jnp.where(same, column, 0.0), 0, keepdims=True)


def weigh_kernel(weight_ref, gain_ref, spread_ref):
    half = spread_ref.shape[2]
    gained = weight_ref[0].astype(f32) * column_of(gain_ref[...].astype(f32))
    gained = gained.astype(bf16)
    for i in range(spread_ref.shape[0]):
        side = i % 2
        spread_ref[i] = gained[:, side * half : (side + 1) * half]


def weigh(weight, gain, copies):
    _, own, out = weight.shape
    return pl.pallas_call(
        weigh_kernel,
        grid=(1,),
        out_shape=jax.ShapeDtypeStruct((2 * copies, own, out // 2), bf16),
        in_specs=[vmem(weight.shape), vmem(gain.shape)],
        out_specs=vmem((2 * copies, own, out // 2)),
        compiler_params=params(40),
        cost_estimate=cost(weight.size, 2 * copies * weight.size),
        name="weigh",
    )(weight, gain)


def stack_kernel(*refs):
    for i, ref in enumerate(refs[:-1]):
        refs[-1][i] = ref[...]


def stack_up(chunks):
    return pl.pallas_call(
        stack_kernel,
        out_shape=jax.ShapeDtypeStruct((len(chunks),) + chunks[0].shape, bf16),
        compiler_params=params(),
        cost_estimate=cost(0, 4 * len(chunks) * chunks[0].size),
        name="stack_up",
    )(*chunks)


def pack_kernel(parts_ref, out_ref):
    count = parts_ref.shape[0]
    for group in range(2):
        rows = [parts_ref[group * count // 2 + i] for i in range(count // 2)]
        span = out_ref.shape[0] // 2
        out_ref[group * span : (group + 1) * span, :] = jnp.concatenate(rows, 0)


def pack(parts):
    count, own, half = parts.shape
    return pl.pallas_call(
        pack_kernel,
        out_shape=jax.ShapeDtypeStruct((count * own, half), bf16),
        compiler_params=params(),
        cost_estimate=cost(0, 4 * parts.size),
        name="pack",
    )(parts)


def partial_kernel(
    core_ref, tokens_ref, others_ref, cot_ref, others_cot_ref, out_ref, mine, theirs
):
    half = mine.shape[1]
    step = out_ref.shape[0]
    place = pl.program_id(0)

    @pl.when(place == 0)
    def _():
        here = pl.ds(pl.multiple_of(core_ref[0] * half, half), half)
        for rows_ref, slopes_ref, shrunk in (
            (tokens_ref, cot_ref, mine), (others_ref, others_cot_ref, theirs)
        ):
            recip = row_recip(rows_ref[...].astype(f32))
            shrunk[...] = (slopes_ref[:, here].astype(f32) * recip).astype(bf16)

    over_rows = (((0,), (0,)), ((), ()))
    lanes = pl.ds(pl.multiple_of(place * step, 128), step)
    first = lax.dot_general(
        tokens_ref[:, lanes], mine[...], over_rows, preferred_element_type=f32
    )
    second = lax.dot_general(
        others_ref[:, lanes], theirs[...], over_rows, preferred_element_type=f32
    )
    out_ref[...] = (first + second).astype(bf16)


def partial_product(core, tokens, others, cotangent, others_cot):
    rows, width = tokens.shape
    out = cotangent.shape[1]
    step = width // 6
    return pl.pallas_call(
        partial_kernel,
        grid=(6,),
        out_shape=jax.ShapeDtypeStruct((width, out // 2), bf16),
        in_specs=[
            pl.BlockSpec(memory_space=pltpu.SMEM),
            vmem((rows, width)),
            vmem((rows, width)),
            vmem((rows, out)),
            vmem((rows, out)),
        ],
        out_specs=pl.BlockSpec((step, out // 2), lambda i: (i, 0)),
        scratch_shapes=[pltpu.VMEM((rows, out // 2), bf16)] * 2,
        compiler_params=params(),
        cost_estimate=cost(2 * rows * width * out, 6 * rows * width),
        name="partial",
    )(core, tokens, others, cotangent, others_cot)


def plane_kernel(parts_ref, out_ref):
    total = parts_ref[0].astype(f32)
    for i in range(1, parts_ref.shape[0]):
        total = total + parts_ref[i].astype(f32)
    own = out_ref.shape[1]
    for i in range(out_ref.shape[0]):
        out_ref[i] = total[i * own : (i + 1) * own].astype(bf16)


def plane_total(parts, owners):
    planes, rows, half = parts.shape
    return pl.pallas_call(
        plane_kernel,
        out_shape=jax.ShapeDtypeStruct((owners, rows // owners, half), bf16),
        compiler_params=params(),
        cost_estimate=cost(parts.size, 3 * parts.size),
        name="plane_total",
    )(parts)


def owner_kernel(factor, blocks_ref, weight_ref, gain_ref, weight_grad_ref, gain_grad_ref):
    half = blocks_ref.shape[2]
    gain = column_of(gain_ref[...].astype(f32))
    dots = 0.0
    for core in range(2):
        total = blocks_ref[core].astype(f32)
        for column in range(1, blocks_ref.shape[0] // 2):
            total = total + blocks_ref[2 * column + core].astype(f32)
        total = total * factor
        columns = slice(core * half, (core + 1) * half)
        weight_grad_ref[:, 0, columns] = total * gain
        dots = dots + jnp.sum(total * weight_ref[0, :, columns].astype(f32), -1, keepdims=True)
    gain_grad_ref[...] = row_of(dots)


def owner_total(factor, blocks, weight, gain):
    return pl.pallas_call(
        functools.partial(owner_kernel, factor),
        out_shape=(
            jax.ShapeDtypeStruct((weight.shape[1], 1, weight.shape[2]), f32),
            jax.ShapeDtypeStruct(gain.shape, f32),
        ),
        compiler_params=params(),
        cost_estimate=cost(blocks.size, 3 * blocks.size),
        name="owner_total",
    )(blocks, weight, gain)


def project_kernel(
    place_ref, tokens_ref, cot_ref, early_ref, late_ref, early_other_ref, late_other_ref,
    layer_ref, grad_ref, whole, product, scaled, stack,
):
    step = pl.program_id(0)
    columns, rows, half = stack.shape
    far = columns // 2
    band = whole.shape[0]
    at, core = place_ref[0], place_ref[1]
    for side, (first, last) in enumerate(
        ((early_ref, late_ref), (early_other_ref, late_other_ref))
    ):
        side_core = core if side == 0 else 1 - core
        stack[:far] = first[:far]
        stack[far] = last[...]
        stack[far + 1 :] = first[far:]
        place = pl.multiple_of(side_core * half, half)
        hops = []
        for y in range(columns):
            hops.append(jnp.where(at < y, at - y + columns, at - y))
        for plane in range(rows // 36):
            span = slice(plane * 36, (plane + 1) * 36)
            piece = jnp.concatenate([stack[hop, span, :] for hop in hops], 0)
            block = columns * 36
            whole[plane * block : (plane + 1) * block, pl.ds(place, half)] = piece
    start = pl.multiple_of(step * band, 128)
    contribution = jnp.dot(
        tokens_ref[:, pl.ds(start, band)], whole[...], preferred_element_type=f32
    )
    scaled[step] = lax.dot_general(
        cot_ref[...], whole[...], (((1,), (1,)), ((), ())), preferred_element_type=f32
    )

    @pl.when(step == 0)
    def _():
        product[...] = contribution

    @pl.when(step == pl.num_programs(0) - 1)
    def _():
        width = tokens_ref.shape[1]
        wide = tokens_ref[...].astype(f32)
        recip = row_recip(wide)
        full = product[...] + contribution
        layer_ref[...] = (full * recip).astype(bf16)
        inner = jnp.sum(full * cot_ref[...].astype(f32), -1, keepdims=True) / width
        slope = recip * recip * recip * inner
        for part in range(2):
            lanes = slice(part * band, (part + 1) * band)
            grad = recip * scaled[part] - tokens_ref[:, lanes].astype(f32) * slope
            grad_ref[:, lanes] = grad.astype(bf16)


def project(place, tokens, cotangent, early, late, early_other, late_other):
    rows, width = tokens.shape
    out = cotangent.shape[1]
    first, per, half = early.shape
    band = width // 2
    return pl.pallas_call(
        project_kernel,
        grid=(2,),
        out_shape=(
            jax.ShapeDtypeStruct((rows, out), bf16),
            jax.ShapeDtypeStruct((rows, width), bf16),
        ),
        in_specs=[
            pl.BlockSpec(memory_space=pltpu.SMEM),
            vmem((rows, width)),
            vmem((rows, out)),
            pl.BlockSpec((first, per // 2, half), lambda i: (0, i, 0)),
            pl.BlockSpec((per // 2, half), lambda i: (i, 0)),
            pl.BlockSpec((first, per // 2, half), lambda i: (0, i, 0)),
            pl.BlockSpec((per // 2, half), lambda i: (i, 0)),
        ],
        out_specs=(vmem((rows, out)), vmem((rows, width))),
        scratch_shapes=[
            pltpu.VMEM((band, out), bf16),
            pltpu.VMEM((rows, out), f32),
            pltpu.VMEM((2, rows, band), f32),
            pltpu.VMEM((first + 1, per // 2, half), bf16),
        ],
        compiler_params=params(48),
        cost_estimate=cost(4 * rows * width * out, 2 * width * out + 4 * rows * (width + out)),
        name="project",
    )(place, tokens, cotangent, early, late, early_other, late_other)


def local(tokens, weight, gain, cotangent, outer_delta, global_params, momentum, plan):
    out = weight.shape[2]
    own, half = weight.shape[1], out // 2
    planes = lax.axis_size("z") * lax.axis_size("x")
    columns = lax.axis_size("y")
    place = jnp.stack([lax.axis_index("y"), lax.axis_index("core")]).astype(jnp.int32)
    core = place[1:]
    replicas = lax.axis_size("rep")
    factor = 1.0 / math.sqrt(tokens.shape[0] * planes * columns * 2)
    after = lax.optimization_barrier

    spread = weigh(weight, gain, planes)
    plane_parts = exchange(spread, ("z", "x", "core"))

    partial = partial_product(core, tokens, swap(tokens), cotangent, swap(cotangent))
    plane = pack(plane_parts)
    received = exchange(partial.reshape(planes, columns * 2 * own, half), ("z", "x"))

    up, down = [plane], [plane]
    for hop in range(1, columns // 2 + 1):
        if hop == columns // 2:
            above, received, below = after((up[-1], received, down[-1]))
            plane_sum = plane_total(received, columns * 2)
            blocks = exchange(plane_sum, ("y", "core"))
            early = stack_up(up + down[:0:-1])
            early_other = swap(early)
            late = turn(above, 1)
        else:
            up.append(turn(up[-1], 1))
            down.append(turn(down[-1], -1))
    weight_grad, gain_grad = owner_total(factor, blocks, weight, gain)
    weight_grad = weight_grad.transpose(1, 0, 2)

    delta, plane_sum = after((outer_delta[0], plane_sum))
    before, behind = cycle(delta, 1), cycle(delta, -1)
    across = cycle(before, 1)
    summed = (delta.astype(f32) + across.astype(f32)) + (before.astype(f32) + behind.astype(f32))

    layer_out, input_grad = project(
        place, tokens, cotangent, early, late, early_other, swap(late)
    )

    chosen = (plan == 1)[:, None, None]
    new_params, new_momentum = outer_step(
        summed / replicas, global_params, momentum, chosen
    )
    return (
        layer_out, input_grad, weight_grad, gain_grad, new_params, new_momentum
    )


def solution(mesh):
    fine = Mesh(mesh.devices.reshape(4, 2, 4, 8, 2), ALL)
    return jax.shard_map(
        local,
        mesh=fine,
        in_specs=(
            P(ALL, None),
            P("rep", FSDP, None),
            P("rep", FSDP),
            P(ALL, None),
            P("rep", None, FSDP, None),
            P(None, FSDP, None),
            P(None, FSDP, None),
            P(),
        ),
        out_specs=(
            P(ALL, None),
            P(ALL, None),
            P("rep", FSDP, None),
            P("rep", FSDP),
            P(None, FSDP, None),
            P(None, FSDP, None),
        ),
        check_vma=False,
    )
```

time: 129 us -> 111 us (0.86)
  the two profiles are of different devices: /device:TPU:1 before, /device:TPU:75 now
where the time goes in v2:
time: 111 us; the launch traced here: 110 us
  starting transfers between devices  67 us (60%)
  waiting for transfers between devices  20.1 us (18%)
  Pallas kernels  16.2 us (15%)
  local copies, waits for them, and re-layouts  3.78 us (3%)
  other arithmetic  2.43 us (2%)
    ppermute x7, starting transfers between devices, turn(): lax.ppermute(values, 'y', [(i, (i + by) % count) for i in range(count)])  20.6 us
    all_to_all x3, starting transfers between devices, exchange(): return lax.all_to_all(values, axes, split_axis=0, concat_axis=0, tiled=True)  18.8 us
    ppermute x3, starting transfers between devices, cycle(): lax.ppermute(values, 'rep', [(i, (i + by) % count) for i in range(count)])  14 us
    ppermute x4, starting transfers between devices, swap(): return lax.ppermute(values, 'core', [(0, 1), (1, 0)])  13.5 us
    ppermute x7, waiting for transfers between devices, turn(): lax.ppermute(values, 'y', [(i, (i + by) % count) for i in range(count)])  11.9 us
    ppermute x3, waiting for transfers between devices, cycle(): lax.ppermute(values, 'rep', [(i, (i + by) % count) for i in range(count)])  8.09 us
    pallas_call x1, Pallas kernels, project(): pl.pallas_call(project_kernel, grid=(2,), out_shape=(jax.ShapeDtypeStruct...  7.51 us
    pallas_call x1, Pallas kernels, partial_product(): pl.pallas_call(partial_kernel, grid=(6,), out_shape=jax.ShapeDtypeStruct(...  4.46 us
  transfers between devices with their start and end apart: 17, of which 8 were waited for; matrix products, arithmetic and copies ran while one was open for 2% of the time, Pallas kernels for 8%

profile of v2, /device:TPU:75, one launch (start us, length us, event | category | flops | bytes accessed | tf_op | source)
XLA Modules:
  0.0 110.4 jit_solution(18119101328439430118)
XLA Ops:
  0.6 2.6 %collective-permute-start.6 = (bf16[256,2304]{1,0:T(8,128)(2,1)}, bf16[256,2304]{1,0:T(8,128)(2,1)S(1)}, u32[]{:S(2)}, u32[]{:S(2)}) collective-permute-start(bf16[256,2304]{1,0:T(8,128)(2,1)} %tokens_ref.3), channel_id=1, source_target_pairs={{0,1},{1,0},{2,3},{3,2},{4,5},{5,4},{6,7},{7,6},{8,9},{9,8},{10,11... | collective-permute-start | bytes 3538952 | tf_op jit(solution)/shard_map/ppermute | solution.py:28
  3.2 1.9 %collective-permute-start.7 = (bf16[256,1024]{1,0:T(8,128)(2,1)}, bf16[256,1024]{1,0:T(8,128)(2,1)S(1)}, u32[]{:S(2)}, u32[]{:S(2)}) collective-permute-start(bf16[256,1024]{1,0:T(8,128)(2,1)} %cot_ref.3), channel_id=1, source_target_pairs={{0,1},{1,0},{2,3},{3,2},{4,5},{5,4},{6,7},{7,6},{8,9},{9,8},{10,11... | collective-permute-start | bytes 1572872 | tf_op jit(solution)/shard_map/ppermute | solution.py:28
  5.2 0.0 copy-start.4
  5.2 0.8 copy-done.4
  6.0 0.0 copy-start.6
  6.0 0.7 copy-done.6
  6.6 0.9 weigh.1
  7.5 5.9 %all-to-all-start = ((bf16[16,18,512]{2,1,0:T(8,128)(2,1)}), bf16[16,18,512]{2,1,0:T(8,128)(2,1)S(1)}, u32[]{:S(2)}, u32[]{:S(2)}) async-start(bf16[16,18,512]{2,1,0:T(8,128)(2,1)} %weigh.1), calls=%async_computation | async-start | bytes 786432 | tf_op jit(solution)/shard_map/all_to_all | solution.py:42
  13.4 0.0 collective-permute-done.7.others_cot_ref
  13.4 0.0 collective-permute-done.6.others_ref
  13.4 0.0 copy-start
  13.4 1.3 %copy-done = bf16[256,2304]{1,0:T(8,128)(2,1)S(1)} copy-done((bf16[256,2304]{1,0:T(8,128)(2,1)S(1)}, bf16[256,2304]{1,0:T(8,128)(2,1)}, u32[]{:S(2)}) %copy-start) | copy-done | bytes 1179672
  14.6 0.0 copy-start.2
  14.6 1.0 copy-done.2
  15.7 4.5 %partial.1 = bf16[2304,512]{1,0:T(8,128)(2,1)} custom-call(s32[1]{0:T(128)} %bitcast.1.core_ref, bf16[256,2304]{1,0:T(8,128)(2,1)S(1)} %copy-done, bf16[256,2304]{1,0:T(8,128)(2,1)S(1)} %collective-permute-done.6.others_ref, bf16[256,1024]{1,0:T(8,128)(2,1)S(1)} %copy-done.2, bf16[256,1024]{1,0:T(8,128)(2,1)S(1)} %collective-permute-done.7.others_cot_ref), custom_call_target="tpu_custom_call" | custom-call | flops 1207959552 | bytes 3538944 | tf_op jit(solution)/shard_map/partial/pallas_call | solution.py:163
  20.1 0.1 all-to-all-done.parts_ref
  20.2 5.1 %all-to-all-start.1 = ((bf16[8,288,512]{2,1,0:T(8,128)(2,1)}), bf16[8,288,512]{2,1,0:T(8,128)(2,1)S(1)}, u32[]{:S(2)}, u32[]{:S(2)}) async-start(bf16[8,288,512]{2,1,0:T(8,128)(2,1)} %bitcast.2), calls=%async_computation.1 | async-start | bytes 4718592 | tf_op jit(solution)/shard_map/all_to_all | solution.py:42
  25.4 4.8 %collective-permute-start.3 = (bf16[288,512]{1,0:T(8,128)(2,1)S(1)}, bf16[288,512]{1,0:T(8,128)(2,1)S(1)}, u32[]{:S(2)}, u32[]{:S(2)}) collective-permute-start(bf16[288,512]{1,0:T(8,128)(2,1)S(1)} %pack.1.refs_0_), channel_id=1, source_target_pairs={{0,14},{2,0},{4,2},{6,4},{8,6},{10,8},{12,10},{14,12},{1,15},{3,1}... | collective-permute-start | bytes 884744 | tf_op jit(solution)/shard_map/ppermute | solution.py:33
  30.2 1.9 %collective-permute-start = (bf16[288,512]{1,0:T(8,128)(2,1)S(1)}, bf16[288,512]{1,0:T(8,128)(2,1)S(1)}, u32[]{:S(2)}, u32[]{:S(2)}) collective-permute-start(bf16[288,512]{1,0:T(8,128)(2,1)S(1)} %pack.1.refs_0_), channel_id=1, source_target_pairs={{0,2},{2,4},{4,6},{6,8},{8,10},{10,12},{12,14},{14,0},{1,3},{3,5},... | collective-permute-start | bytes 884744 | tf_op jit(solution)/shard_map/ppermute | solution.py:33
  32.1 2.9 %collective-permute-done.3.refs_6_ = bf16[288,512]{1,0:T(8,128)(2,1)S(1)} collective-permute-done((bf16[288,512]{1,0:T(8,128)(2,1)S(1)}, bf16[288,512]{1,0:T(8,128)(2,1)S(1)}, u32[]{:S(2)}, u32[]{:S(2)}) %collective-permute-start.3) | collective-permute-done | bytes 294944 | tf_op jit(solution)/shard_map/ppermute | solution.py:33
  35.0 4.1 %collective-permute-start.4 = (bf16[288,512]{1,0:T(8,128)(2,1)S(1)}, bf16[288,512]{1,0:T(8,128)(2,1)S(1)}, u32[]{:S(2)}, u32[]{:S(2)}) collective-permute-start(bf16[288,512]{1,0:T(8,128)(2,1)S(1)} %collective-permute-done.3.refs_6_), channel_id=1, source_target_pairs={{0,14},{2,0},{4,2},{6,4},{8,6},{10,8},{12,10},{14,12},{1,15},{3,1}... | collective-permute-start | bytes 884744 | tf_op jit(solution)/shard_map/ppermute | solution.py:33
  39.1 0.0 collective-permute-done.refs_1_
  39.1 1.9 %collective-permute-start.1 = (bf16[288,512]{1,0:T(8,128)(2,1)S(1)}, bf16[288,512]{1,0:T(8,128)(2,1)S(1)}, u32[]{:S(2)}, u32[]{:S(2)}) collective-permute-start(bf16[288,512]{1,0:T(8,128)(2,1)S(1)} %collective-permute-done.refs_1_), channel_id=1, source_target_pairs={{0,2},{2,4},{4,6},{6,8},{8,10},{10,12},{12,14},{14,0},{1,3},{3,5},... | collective-permute-start | bytes 884744 | tf_op jit(solution)/shard_map/ppermute | solution.py:33
  41.0 2.0 %collective-permute-done.4.refs_5_ = bf16[288,512]{1,0:T(8,128)(2,1)S(1)} collective-permute-done((bf16[288,512]{1,0:T(8,128)(2,1)S(1)}, bf16[288,512]{1,0:T(8,128)(2,1)S(1)}, u32[]{:S(2)}, u32[]{:S(2)}) %collective-permute-start.4) | collective-permute-done | bytes 294944 | tf_op jit(solution)/shard_map/ppermute | solution.py:33
  43.0 4.1 %collective-permute-start.5 = (bf16[288,512]{1,0:T(8,128)(2,1)S(1)}, bf16[288,512]{1,0:T(8,128)(2,1)S(1)}, u32[]{:S(2)}, u32[]{:S(2)}) collective-permute-start(bf16[288,512]{1,0:T(8,128)(2,1)S(1)} %collective-permute-done.4.refs_5_), channel_id=1, source_target_pairs={{0,14},{2,0},{4,2},{6,4},{8,6},{10,8},{12,10},{14,12},{1,15},{3,1}... | collective-permute-start | bytes 884744 | tf_op jit(solution)/shard_map/ppermute | solution.py:33
  47.1 0.3 collective-permute-done.1.refs_2_
  47.4 1.9 %collective-permute-start.2 = (bf16[288,512]{1,0:T(8,128)(2,1)S(1)}, bf16[288,512]{1,0:T(8,128)(2,1)S(1)}, u32[]{:S(2)}, u32[]{:S(2)}) collective-permute-start(bf16[288,512]{1,0:T(8,128)(2,1)S(1)} %collective-permute-done.1.refs_2_), channel_id=1, source_target_pairs={{0,2},{2,4},{4,6},{6,8},{8,10},{10,12},{12,14},{14,0},{1,3},{3,5},... | collective-permute-start | bytes 884744 | tf_op jit(solution)/shard_map/ppermute | solution.py:33
  49.3 2.0 %collective-permute-done.5.refs_4_ = bf16[288,512]{1,0:T(8,128)(2,1)S(1)} collective-permute-done((bf16[288,512]{1,0:T(8,128)(2,1)S(1)}, bf16[288,512]{1,0:T(8,128)(2,1)S(1)}, u32[]{:S(2)}, u32[]{:S(2)}) %collective-permute-start.5) | collective-permute-done | bytes 294944 | tf_op jit(solution)/shard_map/ppermute | solution.py:33
  51.3 4.8 %collective-permute-done.2.refs_3_ = bf16[288,512]{1,0:T(8,128)(2,1)S(1)} collective-permute-done((bf16[288,512]{1,0:T(8,128)(2,1)S(1)}, bf16[288,512]{1,0:T(8,128)(2,1)S(1)}, u32[]{:S(2)}, u32[]{:S(2)}) %collective-permute-start.2) | collective-permute-done | bytes 294944 | tf_op jit(solution)/shard_map/ppermute | solution.py:33
  56.1 1.5 %stack_up.1.early_ref = bf16[7,288,512]{2,1,0:T(8,128)(2,1)} custom-call(bf16[288,512]{1,0:T(8,128)(2,1)S(1)} %pack.1.refs_0_, bf16[288,512]{1,0:T(8,128)(2,1)S(1)} %collective-permute-done.refs_1_, bf16[288,512]{1,0:T(8,128)(2,1)S(1)} %collective-permute-done.1.refs_2_, bf16[288,512]{1,0:T(8,128)(2,1)S(1)} %collective-permute-done.2.refs_3_, ...), custom_call_target="tpu_custom_call" | custom-call | bytes 4128768 | tf_op jit(solution)/shard_map/stack_up/pallas_call | solution.py:104
  57.5 0.0 copy-start.9
  57.6 0.0 copy-start.10
  57.6 0.0 copy-start.8
  57.6 0.0 copy-start.5
  57.6 0.0 copy-start.7
  57.6 6.5 %collective-permute-start.9 = (bf16[7,288,512]{2,1,0:T(8,128)(2,1)}, bf16[7,288,512]{2,1,0:T(8,128)(2,1)}, u32[]{:S(2)}, u32[]{:S(2)}) collective-permute-start(bf16[7,288,512]{2,1,0:T(8,128)(2,1)} %stack_up.1.early_ref), channel_id=1, source_target_pairs={{0,1},{1,0},{2,3},{3,2},{4,5},{5,4},{6,7},{7,6},{8,9},{9,8},{10,11... | collective-permute-start | bytes 6193160 | tf_op jit(solution)/shard_map/ppermute | solution.py:28
  64.1 0.0 all-to-all-done.1.parts_ref
  64.1 1.1 plane_total.1
  65.2 0.0 copy-start.1
  65.2 0.0 copy-start.3
  65.2 0.0 copy-done.9
  65.2 5.9 %collective-permute-start.11 = (bf16[4,18,1024]{2,0,1:T(4,128)(2,1)S(1)}, bf16[4,18,1024]{2,0,1:T(4,128)(2,1)}, u32[]{:S(2)}, u32[]{:S(2)}) collective-permute-start(bf16[4,18,1024]{2,0,1:T(4,128)(2,1)S(1)} %bitcast.5), channel_id=1, source_target_pairs={{0,128},{128,256},{256,384},{384,0},{1,129},{129,257},{257,385},{3... | collective-permute-start | bytes 442376 | tf_op jit(solution)/shard_map/ppermute | solution.py:38
  71.1 1.9 %collective-permute-start.8 = (bf16[288,512]{1,0:T(8,128)(2,1)S(1)}, bf16[288,512]{1,0:T(8,128)(2,1)S(1)}, u32[]{:S(2)}, u32[]{:S(2)}) collective-permute-start(bf16[288,512]{1,0:T(8,128)(2,1)S(1)} %collective-permute-done.2.refs_3_), channel_id=1, source_target_pairs={{0,2},{2,4},{4,6},{6,8},{8,10},{10,12},{12,14},{14,0},{1,3},{3,5},... | collective-permute-start | bytes 884744 | tf_op jit(solution)/shard_map/ppermute | solution.py:33
  73.0 7.8 %all-to-all-start.2 = ((bf16[16,18,512]{2,1,0:T(8,128)(2,1)}), bf16[16,18,512]{2,1,0:T(8,128)(2,1)S(1)}, u32[]{:S(2)}, u32[]{:S(2)}) async-start(bf16[16,18,512]{2,1,0:T(8,128)(2,1)} %plane_total.1), calls=%async_computation.2 | async-start | bytes 786432 | tf_op jit(solution)/shard_map/all_to_all | solution.py:42
  80.8 5.6 %collective-permute-start.13 = (bf16[4,18,1024]{2,0,1:T(4,128)(2,1)S(1)}, bf16[4,18,1024]{2,0,1:T(4,128)(2,1)}, u32[]{:S(2)}, u32[]{:S(2)}) collective-permute-start(bf16[4,18,1024]{2,0,1:T(4,128)(2,1)S(1)} %bitcast.6), channel_id=1, source_target_pairs={{0,384},{128,0},{256,128},{384,256},{1,385},{129,1},{257,129},{385... | collective-permute-start | bytes 442376 | tf_op jit(solution)/shard_map/ppermute | solution.py:38
  86.4 0.0 collective-permute-done.11
  86.4 2.5 %collective-permute-start.12 = (bf16[4,18,1024]{2,0,1:T(4,128)(2,1)}, bf16[4,18,1024]{2,0,1:T(4,128)(2,1)}, u32[]{:S(2)}, u32[]{:S(2)}) collective-permute-start(bf16[4,18,1024]{2,0,1:T(4,128)(2,1)} %collective-permute-done.11), channel_id=1, source_target_pairs={{0,128},{128,256},{256,384},{384,0},{1,129},{129,257},{257,385},{3... | collective-permute-start | bytes 442376 | tf_op jit(solution)/shard_map/ppermute | solution.py:38
  88.9 0.0 copy-done.10
  88.9 0.0 collective-permute-done.8.late_ref
  88.9 2.5 %collective-permute-start.10 = (bf16[288,512]{1,0:T(8,128)(2,1)S(1)}, bf16[288,512]{1,0:T(8,128)(2,1)S(1)}, u32[]{:S(2)}, u32[]{:S(2)}) collective-permute-start(bf16[288,512]{1,0:T(8,128)(2,1)S(1)} %collective-permute-done.8.late_ref), channel_id=1, source_target_pairs={{0,1},{1,0},{2,3},{3,2},{4,5},{5,4},{6,7},{7,6},{8,9},{9,8},{10,11... | collective-permute-start | bytes 884744 | tf_op jit(solution)/shard_map/ppermute | solution.py:28
  91.5 0.1 pad_add_fusion.place_ref
  91.6 2.2 %collective-permute-done.13 = bf16[4,18,1024]{2,0,1:T(4,128)(2,1)} collective-permute-done((bf16[4,18,1024]{2,0,1:T(4,128)(2,1)S(1)}, bf16[4,18,1024]{2,0,1:T(4,128)(2,1)}, u32[]{:S(2)}, u32[]{:S(2)}) %collective-permute-start.13) | collective-permute-done | bytes 147488 | tf_op jit(solution)/shard_map/ppermute | solution.py:38
  93.8 5.9 %collective-permute-done.12 = bf16[4,18,1024]{2,0,1:T(4,128)(2,1)} collective-permute-done((bf16[4,18,1024]{2,0,1:T(4,128)(2,1)}, bf16[4,18,1024]{2,0,1:T(4,128)(2,1)}, u32[]{:S(2)}, u32[]{:S(2)}) %collective-permute-start.12) | collective-permute-done | bytes 147488 | tf_op jit(solution)/shard_map/ppermute | solution.py:38
  99.7 0.0 copy-done.8
  99.7 2.3 %fusion = (f32[4,18,1024]{2,0,1:T(4,128)}, f32[4,18,1024]{2,0,1:T(4,128)}) fusion(f32[4,18,1024]{2,0,1:T(4,128)S(1)} %copy-done.8, pred[4]{0:T(512)(128)(4,1)S(1)} %broadcast_compare_fusion, bf16[4,18,1024]{2,0,1:T(4,128)(2,1)} %collective-permute-done.13, bf16[4,18,1024]{2,0,1:T(4,128)(2,1)} %collective-permute-done.11, ...), kind=kLoop, calls=%fused_computation.2 | loop fusion | flops 1179648 | bytes 1769476 | tf_op jit(solution)/shard_map/jit(_where)/select_n | solution.py:22
  102.0 0.0 all-to-all-done.2.blocks_ref
  102.0 0.0 copy-done.5
  102.0 0.0 copy-done.7
  102.0 0.8 owner_total.1
  102.8 0.0 collective-permute-done.9.early_other_ref
  102.8 0.0 collective-permute-done.10.late_other_ref
  102.8 0.0 copy-done.1
  102.8 0.0 copy-done.3
  102.8 7.5 %project.1 = (bf16[256,1024]{1,0:T(8,128)(2,1)}, bf16[256,2304]{1,0:T(8,128)(2,1)}) custom-call(s32[2]{0:T(128)S(1)} %pad_add_fusion.place_ref, bf16[256,2304]{1,0:T(8,128)(2,1)S(1)} %copy-done.1, bf16[256,1024]{1,0:T(8,128)(2,1)S(1)} %copy-done.3, bf16[7,288,512]{2,1,0:T(8,128)(2,1)} %stack_up.1.early_ref, ...), custom_call_target="tpu_custom_call" | custom-call | flops 2415919104 | bytes 8126464 | tf_op jit(solution)/shard_map/project/pallas_call | solution.py:287
  (2 shorter events, 0.1 us)
Async XLA Ops:
  0.6 12.7 %collective-permute-start.6 = (bf16[256,2304]{1,0:T(8,128)(2,1)}, bf16[256,2304]{1,0:T(8,128)(2,1)S(1)}, u32[]{:S(2)}, u32[]{:S(2)}) collective-permute-start(bf16[256,2304]{1,0:T(8,128)(2,1)} %tokens_ref.3), channel_id=1, source_target_pairs={{0,1},{1,0},{2,3},{3,2},{4,5},{5,4},{6,7},{7,6},{8,9},{9,8},{10,11... | collective-permute-start | bytes 3538952 | tf_op jit(solution)/shard_map/ppermute | solution.py:28
  3.2 10.1 %collective-permute-start.7 = (bf16[256,1024]{1,0:T(8,128)(2,1)}, bf16[256,1024]{1,0:T(8,128)(2,1)S(1)}, u32[]{:S(2)}, u32[]{:S(2)}) collective-permute-start(bf16[256,1024]{1,0:T(8,128)(2,1)} %cot_ref.3), channel_id=1, source_target_pairs={{0,1},{1,0},{2,3},{3,2},{4,5},{5,4},{6,7},{7,6},{8,9},{9,8},{10,11... | collective-permute-start | bytes 1572872 | tf_op jit(solution)/shard_map/ppermute | solution.py:28
  5.2 0.8 copy-start.4
  6.0 0.7 copy-start.6
  7.5 12.8 %all-to-all-start = ((bf16[16,18,512]{2,1,0:T(8,128)(2,1)}), bf16[16,18,512]{2,1,0:T(8,128)(2,1)S(1)}, u32[]{:S(2)}, u32[]{:S(2)}) async-start(bf16[16,18,512]{2,1,0:T(8,128)(2,1)} %weigh.1), calls=%async_computation | async-start | bytes 786432 | tf_op jit(solution)/shard_map/all_to_all | solution.py:42
  13.4 1.3 %copy-start = (bf16[256,2304]{1,0:T(8,128)(2,1)S(1)}, bf16[256,2304]{1,0:T(8,128)(2,1)}, u32[]{:S(2)}) copy-start(bf16[256,2304]{1,0:T(8,128)(2,1)} %tokens_ref.3) | copy-start | bytes 3538948
  14.6 1.0 copy-start.2
  20.2 43.8 %all-to-all-start.1 = ((bf16[8,288,512]{2,1,0:T(8,128)(2,1)}), bf16[8,288,512]{2,1,0:T(8,128)(2,1)S(1)}, u32[]{:S(2)}, u32[]{:S(2)}) async-start(bf16[8,288,512]{2,1,0:T(8,128)(2,1)} %bitcast.2), calls=%async_computation.1 | async-start | bytes 4718592 | tf_op jit(solution)/shard_map/all_to_all | solution.py:42
  25.4 9.6 %collective-permute-start.3 = (bf16[288,512]{1,0:T(8,128)(2,1)S(1)}, bf16[288,512]{1,0:T(8,128)(2,1)S(1)}, u32[]{:S(2)}, u32[]{:S(2)}) collective-permute-start(bf16[288,512]{1,0:T(8,128)(2,1)S(1)} %pack.1.refs_0_), channel_id=1, source_target_pairs={{0,14},{2,0},{4,2},{6,4},{8,6},{10,8},{12,10},{14,12},{1,15},{3,1}... | collective-permute-start | bytes 884744 | tf_op jit(solution)/shard_map/ppermute | solution.py:33
  30.2 8.9 %collective-permute-start = (bf16[288,512]{1,0:T(8,128)(2,1)S(1)}, bf16[288,512]{1,0:T(8,128)(2,1)S(1)}, u32[]{:S(2)}, u32[]{:S(2)}) collective-permute-start(bf16[288,512]{1,0:T(8,128)(2,1)S(1)} %pack.1.refs_0_), channel_id=1, source_target_pairs={{0,2},{2,4},{4,6},{6,8},{8,10},{10,12},{12,14},{14,0},{1,3},{3,5},... | collective-permute-start | bytes 884744 | tf_op jit(solution)/shard_map/ppermute | solution.py:33
  35.0 8.0 %collective-permute-start.4 = (bf16[288,512]{1,0:T(8,128)(2,1)S(1)}, bf16[288,512]{1,0:T(8,128)(2,1)S(1)}, u32[]{:S(2)}, u32[]{:S(2)}) collective-permute-start(bf16[288,512]{1,0:T(8,128)(2,1)S(1)} %collective-permute-done.3.refs_6_), channel_id=1, source_target_pairs={{0,14},{2,0},{4,2},{6,4},{8,6},{10,8},{12,10},{14,12},{1,15},{3,1}... | collective-permute-start | bytes 884744 | tf_op jit(solution)/shard_map/ppermute | solution.py:33
  39.1 8.3 %collective-permute-start.1 = (bf16[288,512]{1,0:T(8,128)(2,1)S(1)}, bf16[288,512]{1,0:T(8,128)(2,1)S(1)}, u32[]{:S(2)}, u32[]{:S(2)}) collective-permute-start(bf16[288,512]{1,0:T(8,128)(2,1)S(1)} %collective-permute-done.refs_1_), channel_id=1, source_target_pairs={{0,2},{2,4},{4,6},{6,8},{8,10},{10,12},{12,14},{14,0},{1,3},{3,5},... | collective-permute-start | bytes 884744 | tf_op jit(solution)/shard_map/ppermute | solution.py:33
  43.0 8.3 %collective-permute-start.5 = (bf16[288,512]{1,0:T(8,128)(2,1)S(1)}, bf16[288,512]{1,0:T(8,128)(2,1)S(1)}, u32[]{:S(2)}, u32[]{:S(2)}) collective-permute-start(bf16[288,512]{1,0:T(8,128)(2,1)S(1)} %collective-permute-done.4.refs_5_), channel_id=1, source_target_pairs={{0,14},{2,0},{4,2},{6,4},{8,6},{10,8},{12,10},{14,12},{1,15},{3,1}... | collective-permute-start | bytes 884744 | tf_op jit(solution)/shard_map/ppermute | solution.py:33
  47.4 8.7 %collective-permute-start.2 = (bf16[288,512]{1,0:T(8,128)(2,1)S(1)}, bf16[288,512]{1,0:T(8,128)(2,1)S(1)}, u32[]{:S(2)}, u32[]{:S(2)}) collective-permute-start(bf16[288,512]{1,0:T(8,128)(2,1)S(1)} %collective-permute-done.1.refs_2_), channel_id=1, source_target_pairs={{0,2},{2,4},{4,6},{6,8},{8,10},{10,12},{12,14},{14,0},{1,3},{3,5},... | collective-permute-start | bytes 884744 | tf_op jit(solution)/shard_map/ppermute | solution.py:33
  57.5 7.6 %copy-start.9 = (bf16[1,4,18,1024]{3,1,2,0:T(4,128)(2,1)S(1)}, bf16[1,4,18,1024]{3,1,2,0:T(4,128)(2,1)}, u32[]{:S(2)}) copy-start(bf16[1,4,18,1024]{3,1,2,0:T(4,128)(2,1)} %param.12) | copy-start | bytes 442372
  57.6 31.3 %copy-start.10 = (s32[4]{0:T(128)S(1)}, s32[4]{0:T(128)}, u32[]{:S(2)}) copy-start(s32[4]{0:T(128)} %param.15) | copy-start | bytes 52
  57.6 42.1 %copy-start.8 = (f32[4,18,1024]{2,0,1:T(4,128)S(1)}, f32[4,18,1024]{2,0,1:T(4,128)}, u32[]{:S(2)}) copy-start(f32[4,18,1024]{2,0,1:T(4,128)} %param.14) | copy-start | bytes 884740
  57.6 44.5 %copy-start.5 = (bf16[1,18,1024]{2,1,0:T(8,128)(2,1)S(1)}, bf16[1,18,1024]{2,1,0:T(8,128)(2,1)}, u32[]{:S(2)}) copy-start(bf16[1,18,1024]{2,1,0:T(8,128)(2,1)} %weight_ref.3) | copy-start | bytes 110596
  57.6 44.5 %copy-start.7 = (bf16[1,18]{1,0:T(2,128)(2,1)S(1)}, bf16[1,18]{1,0:T(2,128)(2,1)}, u32[]{:S(2)}) copy-start(bf16[1,18]{1,0:T(2,128)(2,1)} %gain_ref.3) | copy-start | bytes 112
  57.6 45.2 %collective-permute-start.9 = (bf16[7,288,512]{2,1,0:T(8,128)(2,1)}, bf16[7,288,512]{2,1,0:T(8,128)(2,1)}, u32[]{:S(2)}, u32[]{:S(2)}) collective-permute-start(bf16[7,288,512]{2,1,0:T(8,128)(2,1)} %stack_up.1.early_ref), channel_id=1, source_target_pairs={{0,1},{1,0},{2,3},{3,2},{4,5},{5,4},{6,7},{7,6},{8,9},{9,8},{10,11... | collective-permute-start | bytes 6193160 | tf_op jit(solution)/shard_map/ppermute | solution.py:28
  65.2 37.7 %copy-start.1 = (bf16[256,2304]{1,0:T(8,128)(2,1)S(1)}, bf16[256,2304]{1,0:T(8,128)(2,1)}, u32[]{:S(2)}) copy-start(bf16[256,2304]{1,0:T(8,128)(2,1)} %tokens_ref.3) | copy-start | bytes 3538948
  65.2 37.7 %copy-start.3 = (bf16[256,1024]{1,0:T(8,128)(2,1)S(1)}, bf16[256,1024]{1,0:T(8,128)(2,1)}, u32[]{:S(2)}) copy-start(bf16[256,1024]{1,0:T(8,128)(2,1)} %cot_ref.3) | copy-start | bytes 1572868
  65.2 21.3 %collective-permute-start.11 = (bf16[4,18,1024]{2,0,1:T(4,128)(2,1)S(1)}, bf16[4,18,1024]{2,0,1:T(4,128)(2,1)}, u32[]{:S(2)}, u32[]{:S(2)}) collective-permute-start(bf16[4,18,1024]{2,0,1:T(4,128)(2,1)S(1)} %bitcast.5), channel_id=1, source_target_pairs={{0,128},{128,256},{256,384},{384,0},{1,129},{129,257},{257,385},{3... | collective-permute-start | bytes 442376 | tf_op jit(solution)/shard_map/ppermute | solution.py:38
  71.1 17.8 %collective-permute-start.8 = (bf16[288,512]{1,0:T(8,128)(2,1)S(1)}, bf16[288,512]{1,0:T(8,128)(2,1)S(1)}, u32[]{:S(2)}, u32[]{:S(2)}) collective-permute-start(bf16[288,512]{1,0:T(8,128)(2,1)S(1)} %collective-permute-done.2.refs_3_), channel_id=1, source_target_pairs={{0,2},{2,4},{4,6},{6,8},{8,10},{10,12},{12,14},{14,0},{1,3},{3,5},... | collective-permute-start | bytes 884744 | tf_op jit(solution)/shard_map/ppermute | solution.py:33
  73.0 29.0 %all-to-all-start.2 = ((bf16[16,18,512]{2,1,0:T(8,128)(2,1)}), bf16[16,18,512]{2,1,0:T(8,128)(2,1)S(1)}, u32[]{:S(2)}, u32[]{:S(2)}) async-start(bf16[16,18,512]{2,1,0:T(8,128)(2,1)} %plane_total.1), calls=%async_computation.2 | async-start | bytes 786432 | tf_op jit(solution)/shard_map/all_to_all | solution.py:42
  80.8 12.9 %collective-permute-start.13 = (bf16[4,18,1024]{2,0,1:T(4,128)(2,1)S(1)}, bf16[4,18,1024]{2,0,1:T(4,128)(2,1)}, u32[]{:S(2)}, u32[]{:S(2)}) collective-permute-start(bf16[4,18,1024]{2,0,1:T(4,128)(2,1)S(1)} %bitcast.6), channel_id=1, source_target_pairs={{0,384},{128,0},{256,128},{384,256},{1,385},{129,1},{257,129},{385... | collective-permute-start | bytes 442376 | tf_op jit(solution)/shard_map/ppermute | solution.py:38
  86.4 13.2 %collective-permute-start.12 = (bf16[4,18,1024]{2,0,1:T(4,128)(2,1)}, bf16[4,18,1024]{2,0,1:T(4,128)(2,1)}, u32[]{:S(2)}, u32[]{:S(2)}) collective-permute-start(bf16[4,18,1024]{2,0,1:T(4,128)(2,1)} %collective-permute-done.11), channel_id=1, source_target_pairs={{0,128},{128,256},{256,384},{384,0},{1,129},{129,257},{257,385},{3... | collective-permute-start | bytes 442376 | tf_op jit(solution)/shard_map/ppermute | solution.py:38
  88.9 13.9 %collective-permute-start.10 = (bf16[288,512]{1,0:T(8,128)(2,1)S(1)}, bf16[288,512]{1,0:T(8,128)(2,1)S(1)}, u32[]{:S(2)}, u32[]{:S(2)}) collective-permute-start(bf16[288,512]{1,0:T(8,128)(2,1)S(1)} %collective-permute-done.8.late_ref), channel_id=1, source_target_pairs={{0,1},{1,0},{2,3},{3,2},{4,5},{5,4},{6,7},{7,6},{8,9},{9,8},{10,11... | collective-permute-start | bytes 884744 | tf_op jit(solution)/shard_map/ppermute | solution.py:28

commit v3 on v2

--- a/solution.py
+++ b/solution.py
@@ -33,9 +33,8 @@
     return lax.ppermute(values, "y", [(i, (i + by) % count) for i in range(count)])
 
 
-def cycle(values, by):
-    count = lax.axis_size("rep")
-    return lax.ppermute(values, "rep", [(i, (i + by) % count) for i in range(count)])
+def partner(values, partners):
+    return lax.ppermute(values, "rep", list(enumerate(partners)))
 
 
 def exchange(values, axes):
@@ -327,7 +326,8 @@
     spread = weigh(weight, gain, planes)
     plane_parts = exchange(spread, ("z", "x", "core"))
 
-    partial = partial_product(core, tokens, swap(tokens), cotangent, swap(cotangent))
+    ready_tokens, ready_cot, _ = after((tokens, cotangent, spread))
+    partial = partial_product(core, tokens, swap(ready_tokens), cotangent, swap(ready_cot))
     plane = pack(plane_parts)
     received = exchange(partial.reshape(planes, columns * 2 * own, half), ("z", "x"))
 
@@ -343,17 +343,20 @@
         else:
             up.append(turn(up[-1], 1))
             down.append(turn(down[-1], -1))
+
+    delta, plane_sum = after((outer_delta[0], plane_sum))
+    pair = (delta.astype(f32) + partner(delta, (1, 0, 3, 2)).astype(f32)).astype(bf16)
+    pair, late = after((pair, late))
+    other_pair = partner(pair, (3, 2, 1, 0))
+
+    layer_out, input_grad = project(
+        place, tokens, cotangent, early, late, early_other, swap(late)
+    )
+
+    layer_out, other_pair, blocks = after((layer_out, other_pair, blocks))
+    summed = pair.astype(f32) + other_pair.astype(f32)
     weight_grad, gain_grad = owner_total(factor, blocks, weight, gain)
     weight_grad = weight_grad.transpose(1, 0, 2)
-
-    delta, plane_sum = after((outer_delta[0], plane_sum))
-    before, behind = cycle(delta, 1), cycle(delta, -1)
-    across = cycle(before, 1)
-    summed = (delta.astype(f32) + across.astype(f32)) + (before.astype(f32) + behind.astype(f32))
-
-    layer_out, input_grad = project(
-        place, tokens, cotangent, early, late, early_other, swap(late)
-    )
 
     chosen = (plan == 1)[:, None, None]
     new_params, new_momentum = outer_step(

time: 111 us -> 110 us (level)
  the two profiles are of different devices: /device:TPU:75 before, /device:TPU:25 now
where the time goes in v3:
time: 110 us; the launch traced here: 109 us
  starting transfers between devices  66.7 us (61%)
  Pallas kernels  17.3 us (16%)
  waiting for transfers between devices  17.2 us (16%)
  local copies, waits for them, and re-layouts  4.81 us (4%)
  other arithmetic  2.18 us (2%)
    ppermute x7, starting transfers between devices, turn(): lax.ppermute(values, 'y', [(i, (i + by) % count) for i in range(count)])  22.7 us
    ppermute x4, starting transfers between devices, swap(): return lax.ppermute(values, 'core', [(0, 1), (1, 0)])  16.2 us
    all_to_all x3, starting transfers between devices, exchange(): return lax.all_to_all(values, axes, split_axis=0, concat_axis=0, tiled=True)  15.9 us
    ppermute x7, waiting for transfers between devices, turn(): lax.ppermute(values, 'y', [(i, (i + by) % count) for i in range(count)])  15.6 us
    ppermute x2, starting transfers between devices, partner(): return lax.ppermute(values, 'rep', list(enumerate(partners)))  11.9 us
    pallas_call x1, Pallas kernels, project(): pl.pallas_call(project_kernel, grid=(2,), out_shape=(jax.ShapeDtypeStruct...  7.61 us
    unnamed x22, local copies, waits for them, and re-layouts  4.81 us
    pallas_call x1, Pallas kernels, partial_product(): pl.pallas_call(partial_kernel, grid=(6,), out_shape=jax.ShapeDtypeStruct(...  4.47 us
  transfers between devices with their start and end apart: 16, of which 6 were waited for; matrix products, arithmetic and copies ran while one was open for 1% of the time, Pallas kernels for 14%

profile of v3, /device:TPU:25, one launch (start us, length us, event | category | flops | bytes accessed | tf_op | source)
XLA Modules:
  0.0 109.1 jit_solution(9271196620934430883)
XLA Ops:
  0.6 0.0 copy-start.4
  0.6 0.8 copy-done.4
  1.4 0.0 copy-start.6
  1.4 0.7 copy-done.6
  2.1 0.9 weigh.1
  2.9 2.6 %collective-permute-start.6 = (bf16[256,2304]{1,0:T(8,128)(2,1)}, bf16[256,2304]{1,0:T(8,128)(2,1)S(1)}, u32[]{:S(2)}, u32[]{:S(2)}) collective-permute-start(bf16[256,2304]{1,0:T(8,128)(2,1)} %tokens_ref.3), channel_id=1, source_target_pairs={{0,1},{1,0},{2,3},{3,2},{4,5},{5,4},{6,7},{7,6},{8,9},{9,8},{10,11... | collective-permute-start | bytes 3538952 | tf_op jit(solution)/shard_map/ppermute | solution.py:28
  5.5 1.9 %collective-permute-start.7 = (bf16[256,1024]{1,0:T(8,128)(2,1)}, bf16[256,1024]{1,0:T(8,128)(2,1)S(1)}, u32[]{:S(2)}, u32[]{:S(2)}) collective-permute-start(bf16[256,1024]{1,0:T(8,128)(2,1)} %cot_ref.3), channel_id=1, source_target_pairs={{0,1},{1,0},{2,3},{3,2},{4,5},{5,4},{6,7},{7,6},{8,9},{9,8},{10,11... | collective-permute-start | bytes 1572872 | tf_op jit(solution)/shard_map/ppermute | solution.py:28
  7.5 6.6 %all-to-all-start = ((bf16[16,18,512]{2,1,0:T(8,128)(2,1)}), bf16[16,18,512]{2,1,0:T(8,128)(2,1)S(1)}, u32[]{:S(2)}, u32[]{:S(2)}) async-start(bf16[16,18,512]{2,1,0:T(8,128)(2,1)} %weigh.1), calls=%async_computation | async-start | bytes 786432 | tf_op jit(solution)/shard_map/all_to_all | solution.py:41
  14.1 0.0 collective-permute-done.7.others_cot_ref
  14.1 0.0 collective-permute-done.6.others_ref
  14.1 0.0 copy-start
  14.1 1.3 %copy-done = bf16[256,2304]{1,0:T(8,128)(2,1)S(1)} copy-done((bf16[256,2304]{1,0:T(8,128)(2,1)S(1)}, bf16[256,2304]{1,0:T(8,128)(2,1)}, u32[]{:S(2)}) %copy-start) | copy-done | bytes 1179672
  15.4 0.0 copy-start.2
  15.4 1.0 copy-done.2
  16.4 4.5 %partial.1 = bf16[2304,512]{1,0:T(8,128)(2,1)} custom-call(s32[1]{0:T(128)} %bitcast.1.core_ref, bf16[256,2304]{1,0:T(8,128)(2,1)S(1)} %copy-done, bf16[256,2304]{1,0:T(8,128)(2,1)S(1)} %collective-permute-done.6.others_ref, bf16[256,1024]{1,0:T(8,128)(2,1)S(1)} %copy-done.2, bf16[256,1024]{1,0:T(8,128)(2,1)S(1)} %collective-permute-done.7.others_cot_ref), custom_call_target="tpu_custom_call" | custom-call | flops 1207959552 | bytes 3538944 | tf_op jit(solution)/shard_map/partial/pallas_call | solution.py:162
  20.9 1.6 %all-to-all-done.parts_ref = bf16[16,18,512]{2,1,0:T(8,128)(2,1)S(1)} async-done(((bf16[16,18,512]{2,1,0:T(8,128)(2,1)}), bf16[16,18,512]{2,1,0:T(8,128)(2,1)S(1)}, u32[]{:S(2)}, u32[]{:S(2)}) %all-to-all-start) | async-done | bytes 294944 | tf_op jit(solution)/shard_map/all_to_all | solution.py:41
  22.5 3.6 %all-to-all-start.1 = ((bf16[8,288,512]{2,1,0:T(8,128)(2,1)}), bf16[8,288,512]{2,1,0:T(8,128)(2,1)S(1)}, u32[]{:S(2)}, u32[]{:S(2)}) async-start(bf16[8,288,512]{2,1,0:T(8,128)(2,1)} %bitcast.3), calls=%async_computation.1 | async-start | bytes 4718592 | tf_op jit(solution)/shard_map/all_to_all | solution.py:41
  26.2 4.4 %collective-permute-start = (bf16[288,512]{1,0:T(8,128)(2,1)S(1)}, bf16[288,512]{1,0:T(8,128)(2,1)S(1)}, u32[]{:S(2)}, u32[]{:S(2)}) collective-permute-start(bf16[288,512]{1,0:T(8,128)(2,1)S(1)} %pack.1.refs_0_), channel_id=1, source_target_pairs={{0,2},{2,4},{4,6},{6,8},{8,10},{10,12},{12,14},{14,0},{1,3},{3,5},... | collective-permute-start | bytes 884744 | tf_op jit(solution)/shard_map/ppermute | solution.py:33
  30.6 1.9 %collective-permute-start.3 = (bf16[288,512]{1,0:T(8,128)(2,1)S(1)}, bf16[288,512]{1,0:T(8,128)(2,1)S(1)}, u32[]{:S(2)}, u32[]{:S(2)}) collective-permute-start(bf16[288,512]{1,0:T(8,128)(2,1)S(1)} %pack.1.refs_0_), channel_id=1, source_target_pairs={{0,14},{2,0},{4,2},{6,4},{8,6},{10,8},{12,10},{14,12},{1,15},{3,1}... | collective-permute-start | bytes 884744 | tf_op jit(solution)/shard_map/ppermute | solution.py:33
  32.5 3.2 %collective-permute-done.refs_1_ = bf16[288,512]{1,0:T(8,128)(2,1)S(1)} collective-permute-done((bf16[288,512]{1,0:T(8,128)(2,1)S(1)}, bf16[288,512]{1,0:T(8,128)(2,1)S(1)}, u32[]{:S(2)}, u32[]{:S(2)}) %collective-permute-start) | collective-permute-done | bytes 294944 | tf_op jit(solution)/shard_map/ppermute | solution.py:33
  35.7 5.3 %collective-permute-start.1 = (bf16[288,512]{1,0:T(8,128)(2,1)S(1)}, bf16[288,512]{1,0:T(8,128)(2,1)S(1)}, u32[]{:S(2)}, u32[]{:S(2)}) collective-permute-start(bf16[288,512]{1,0:T(8,128)(2,1)S(1)} %collective-permute-done.refs_1_), channel_id=1, source_target_pairs={{0,2},{2,4},{4,6},{6,8},{8,10},{10,12},{12,14},{14,0},{1,3},{3,5},... | collective-permute-start | bytes 884744 | tf_op jit(solution)/shard_map/ppermute | solution.py:33
  41.0 0.0 collective-permute-done.3.refs_6_
  41.0 1.9 %collective-permute-start.4 = (bf16[288,512]{1,0:T(8,128)(2,1)S(1)}, bf16[288,512]{1,0:T(8,128)(2,1)S(1)}, u32[]{:S(2)}, u32[]{:S(2)}) collective-permute-start(bf16[288,512]{1,0:T(8,128)(2,1)S(1)} %collective-permute-done.3.refs_6_), channel_id=1, source_target_pairs={{0,14},{2,0},{4,2},{6,4},{8,6},{10,8},{12,10},{14,12},{1,15},{3,1}... | collective-permute-start | bytes 884744 | tf_op jit(solution)/shard_map/ppermute | solution.py:33
  42.9 2.2 %collective-permute-done.1.refs_2_ = bf16[288,512]{1,0:T(8,128)(2,1)S(1)} collective-permute-done((bf16[288,512]{1,0:T(8,128)(2,1)S(1)}, bf16[288,512]{1,0:T(8,128)(2,1)S(1)}, u32[]{:S(2)}, u32[]{:S(2)}) %collective-permute-start.1) | collective-permute-done | bytes 294944 | tf_op jit(solution)/shard_map/ppermute | solution.py:33
  45.2 5.3 %collective-permute-start.2 = (bf16[288,512]{1,0:T(8,128)(2,1)S(1)}, bf16[288,512]{1,0:T(8,128)(2,1)}, u32[]{:S(2)}, u32[]{:S(2)}) collective-permute-start(bf16[288,512]{1,0:T(8,128)(2,1)S(1)} %collective-permute-done.1.refs_2_), channel_id=1, source_target_pairs={{0,2},{2,4},{4,6},{6,8},{8,10},{10,12},{12,14},{14,0},{1,3},{3,5},... | collective-permute-start | bytes 884744 | tf_op jit(solution)/shard_map/ppermute | solution.py:33
  50.5 0.0 collective-permute-done.4.refs_5_
  50.5 1.9 %collective-permute-start.5 = (bf16[288,512]{1,0:T(8,128)(2,1)S(1)}, bf16[288,512]{1,0:T(8,128)(2,1)S(1)}, u32[]{:S(2)}, u32[]{:S(2)}) collective-permute-start(bf16[288,512]{1,0:T(8,128)(2,1)S(1)} %collective-permute-done.4.refs_5_), channel_id=1, source_target_pairs={{0,14},{2,0},{4,2},{6,4},{8,6},{10,8},{12,10},{14,12},{1,15},{3,1}... | collective-permute-start | bytes 884744 | tf_op jit(solution)/shard_map/ppermute | solution.py:33
  52.4 1.7 %collective-permute-done.2.refs_3_ = bf16[288,512]{1,0:T(8,128)(2,1)} collective-permute-done((bf16[288,512]{1,0:T(8,128)(2,1)S(1)}, bf16[288,512]{1,0:T(8,128)(2,1)}, u32[]{:S(2)}, u32[]{:S(2)}) %collective-permute-start.2) | collective-permute-done | bytes 294944 | tf_op jit(solution)/shard_map/ppermute | solution.py:33
  54.2 5.0 %collective-permute-done.5.refs_4_ = bf16[288,512]{1,0:T(8,128)(2,1)S(1)} collective-permute-done((bf16[288,512]{1,0:T(8,128)(2,1)S(1)}, bf16[288,512]{1,0:T(8,128)(2,1)S(1)}, u32[]{:S(2)}, u32[]{:S(2)}) %collective-permute-start.5) | collective-permute-done | bytes 294944 | tf_op jit(solution)/shard_map/ppermute | solution.py:33
  59.2 2.4 %stack_up.1.early_ref = bf16[7,288,512]{2,1,0:T(8,128)(2,1)} custom-call(bf16[288,512]{1,0:T(8,128)(2,1)S(1)} %pack.1.refs_0_, bf16[288,512]{1,0:T(8,128)(2,1)S(1)} %collective-permute-done.refs_1_, bf16[288,512]{1,0:T(8,128)(2,1)S(1)} %collective-permute-done.1.refs_2_, bf16[288,512]{1,0:T(8,128)(2,1)} %collective-permute-done.2.refs_3_, ...), custom_call_target="tpu_custom_call" | custom-call | bytes 4128768 | tf_op jit(solution)/shard_map/stack_up/pallas_call | solution.py:103
  61.6 0.0 copy-start.10
  61.6 0.0 copy-start.1
  61.6 6.5 %collective-permute-start.10 = (bf16[7,288,512]{2,1,0:T(8,128)(2,1)}, bf16[7,288,512]{2,1,0:T(8,128)(2,1)}, u32[]{:S(2)}, u32[]{:S(2)}) collective-permute-start(bf16[7,288,512]{2,1,0:T(8,128)(2,1)} %stack_up.1.early_ref), channel_id=1, source_target_pairs={{0,1},{1,0},{2,3},{3,2},{4,5},{5,4},{6,7},{7,6},{8,9},{9,8},{10,11... | collective-permute-start | bytes 6193160 | tf_op jit(solution)/shard_map/ppermute | solution.py:28
  68.1 0.0 all-to-all-done.1.parts_ref
  68.1 1.1 plane_total.1
  69.2 5.8 %collective-permute-start.8 = (bf16[4,18,1024]{2,0,1:T(4,128)(2,1)}, bf16[4,18,1024]{2,0,1:T(4,128)(2,1)S(1)}, u32[]{:S(2)}, u32[]{:S(2)}) collective-permute-start(bf16[4,18,1024]{2,0,1:T(4,128)(2,1)} %bitcast.2), channel_id=1, source_target_pairs={{0,128},{128,0},{256,384},{384,256},{1,129},{129,1},{257,385},{385... | collective-permute-start | bytes 442376 | tf_op jit(solution)/shard_map/ppermute | solution.py:37
  75.0 1.9 %collective-permute-start.9 = (bf16[288,512]{1,0:T(8,128)(2,1)}, bf16[288,512]{1,0:T(8,128)(2,1)S(1)}, u32[]{:S(2)}, u32[]{:S(2)}) collective-permute-start(bf16[288,512]{1,0:T(8,128)(2,1)} %collective-permute-done.2.refs_3_), channel_id=1, source_target_pairs={{0,2},{2,4},{4,6},{6,8},{8,10},{10,12},{12,14},{14,0},{1,3},{3,5},... | collective-permute-start | bytes 884744 | tf_op jit(solution)/shard_map/ppermute | solution.py:33
  76.9 5.6 %all-to-all-start.2 = ((bf16[16,18,512]{2,1,0:T(8,128)(2,1)}), bf16[16,18,512]{2,1,0:T(8,128)(2,1)S(1)}, u32[]{:S(2)}, u32[]{:S(2)}) async-start(bf16[16,18,512]{2,1,0:T(8,128)(2,1)} %plane_total.1), calls=%async_computation.2 | async-start | bytes 786432 | tf_op jit(solution)/shard_map/all_to_all | solution.py:41
  82.5 0.0 collective-permute-done.8
  82.6 1.0 add_convert_fusion
  83.6 3.4 %collective-permute-done.9.late_ref = bf16[288,512]{1,0:T(8,128)(2,1)S(1)} collective-permute-done((bf16[288,512]{1,0:T(8,128)(2,1)}, bf16[288,512]{1,0:T(8,128)(2,1)S(1)}, u32[]{:S(2)}, u32[]{:S(2)}) %collective-permute-start.9) | collective-permute-done | bytes 294944 | tf_op jit(solution)/shard_map/ppermute | solution.py:33
  87.0 5.3 %collective-permute-start.11 = (bf16[288,512]{1,0:T(8,128)(2,1)S(1)}, bf16[288,512]{1,0:T(8,128)(2,1)S(1)}, u32[]{:S(2)}, u32[]{:S(2)}) collective-permute-start(bf16[288,512]{1,0:T(8,128)(2,1)S(1)} %collective-permute-done.9.late_ref), channel_id=1, source_target_pairs={{0,1},{1,0},{2,3},{3,2},{4,5},{5,4},{6,7},{7,6},{8,9},{9,8},{10,11... | collective-permute-start | bytes 884744 | tf_op jit(solution)/shard_map/ppermute | solution.py:28
  92.3 0.1 pad_add_fusion.place_ref
  92.3 0.0 copy-done.10
  92.3 0.0 copy-start.7
  92.4 6.1 %collective-permute-start.12 = (bf16[4,18,1024]{2,0,1:T(4,128)(2,1)S(1)}, bf16[4,18,1024]{2,0,1:T(4,128)(2,1)S(1)}, u32[]{:S(2)}, u32[]{:S(2)}) collective-permute-start(bf16[4,18,1024]{2,0,1:T(4,128)(2,1)S(1)} %add_convert_fusion), channel_id=1, source_target_pairs={{0,384},{128,256},{256,128},{384,0},{1,385},{129,257},{257,129},{3... | collective-permute-start | bytes 442376 | tf_op jit(solution)/shard_map/ppermute | solution.py:37
  98.5 0.0 collective-permute-done.10.early_other_ref
  98.5 0.0 collective-permute-done.11.late_other_ref
  98.5 0.0 copy-done.1
  98.5 0.0 copy-start.3
  98.5 1.0 copy-done.3
  99.6 0.0 copy-start.5
  99.6 0.0 copy-start.8
  99.6 0.0 copy-start.9
  99.6 7.6 %project.1 = (bf16[256,1024]{1,0:T(8,128)(2,1)}, bf16[256,2304]{1,0:T(8,128)(2,1)}) custom-call(s32[2]{0:T(128)S(1)} %pad_add_fusion.place_ref, bf16[256,2304]{1,0:T(8,128)(2,1)S(1)} %copy-done.1, bf16[256,1024]{1,0:T(8,128)(2,1)S(1)} %copy-done.3, bf16[7,288,512]{2,1,0:T(8,128)(2,1)} %stack_up.1.early_ref, ...), custom_call_target="tpu_custom_call" | custom-call | flops 2415919104 | bytes 8126464 | tf_op jit(solution)/shard_map/project/pallas_call | solution.py:286
  107.2 0.0 collective-permute-done.12
  107.2 0.0 all-to-all-done.2.blocks_ref
  107.2 0.0 copy-done.7
  107.2 0.0 copy-done.5
  107.2 0.8 owner_total.1
  108.0 0.0 copy-done.8
  108.0 0.0 copy-done.9
  108.0 1.1 %fusion = (f32[4,18,1024]{2,0,1:T(4,128)}, f32[4,18,1024]{2,0,1:T(4,128)}) fusion(f32[4,18,1024]{2,0,1:T(4,128)S(1)} %copy-done.8, bf16[4,18,1024]{2,0,1:T(4,128)(2,1)S(1)} %collective-permute-done.12, bf16[4,18,1024]{2,0,1:T(4,128)(2,1)S(1)} %add_convert_fusion, pred[4]{0:T(512)(128)(4,1)S(1)} %broadcast_compare_fusion, f32[4,18,1024]{2,0,1:T(4,128)S(1)} %copy-done.9), kind=kLoop, calls=%fused_computation.2 | loop fusion | flops 884736 | bytes 1474564 | tf_op jit(solution)/shard_map/jit(_where)/select_n | solution.py:22
  (2 shorter events, 0.1 us)
Async XLA Ops:
  0.6 0.8 copy-start.4
  1.4 0.7 copy-start.6
  2.9 11.2 %collective-permute-start.6 = (bf16[256,2304]{1,0:T(8,128)(2,1)}, bf16[256,2304]{1,0:T(8,128)(2,1)S(1)}, u32[]{:S(2)}, u32[]{:S(2)}) collective-permute-start(bf16[256,2304]{1,0:T(8,128)(2,1)} %tokens_ref.3), channel_id=1, source_target_pairs={{0,1},{1,0},{2,3},{3,2},{4,5},{5,4},{6,7},{7,6},{8,9},{9,8},{10,11... | collective-permute-start | bytes 3538952 | tf_op jit(solution)/shard_map/ppermute | solution.py:28
  5.5 8.6 %collective-permute-start.7 = (bf16[256,1024]{1,0:T(8,128)(2,1)}, bf16[256,1024]{1,0:T(8,128)(2,1)S(1)}, u32[]{:S(2)}, u32[]{:S(2)}) collective-permute-start(bf16[256,1024]{1,0:T(8,128)(2,1)} %cot_ref.3), channel_id=1, source_target_pairs={{0,1},{1,0},{2,3},{3,2},{4,5},{5,4},{6,7},{7,6},{8,9},{9,8},{10,11... | collective-permute-start | bytes 1572872 | tf_op jit(solution)/shard_map/ppermute | solution.py:28
  7.5 15.0 %all-to-all-start = ((bf16[16,18,512]{2,1,0:T(8,128)(2,1)}), bf16[16,18,512]{2,1,0:T(8,128)(2,1)S(1)}, u32[]{:S(2)}, u32[]{:S(2)}) async-start(bf16[16,18,512]{2,1,0:T(8,128)(2,1)} %weigh.1), calls=%async_computation | async-start | bytes 786432 | tf_op jit(solution)/shard_map/all_to_all | solution.py:41
  14.1 1.3 %copy-start = (bf16[256,2304]{1,0:T(8,128)(2,1)S(1)}, bf16[256,2304]{1,0:T(8,128)(2,1)}, u32[]{:S(2)}) copy-start(bf16[256,2304]{1,0:T(8,128)(2,1)} %tokens_ref.3) | copy-start | bytes 3538948
  15.4 1.0 copy-start.2
  22.5 45.6 %all-to-all-start.1 = ((bf16[8,288,512]{2,1,0:T(8,128)(2,1)}), bf16[8,288,512]{2,1,0:T(8,128)(2,1)S(1)}, u32[]{:S(2)}, u32[]{:S(2)}) async-start(bf16[8,288,512]{2,1,0:T(8,128)(2,1)} %bitcast.3), calls=%async_computation.1 | async-start | bytes 4718592 | tf_op jit(solution)/shard_map/all_to_all | solution.py:41
  26.2 9.5 %collective-permute-start = (bf16[288,512]{1,0:T(8,128)(2,1)S(1)}, bf16[288,512]{1,0:T(8,128)(2,1)S(1)}, u32[]{:S(2)}, u32[]{:S(2)}) collective-permute-start(bf16[288,512]{1,0:T(8,128)(2,1)S(1)} %pack.1.refs_0_), channel_id=1, source_target_pairs={{0,2},{2,4},{4,6},{6,8},{8,10},{10,12},{12,14},{14,0},{1,3},{3,5},... | collective-permute-start | bytes 884744 | tf_op jit(solution)/shard_map/ppermute | solution.py:33
  30.6 10.4 %collective-permute-start.3 = (bf16[288,512]{1,0:T(8,128)(2,1)S(1)}, bf16[288,512]{1,0:T(8,128)(2,1)S(1)}, u32[]{:S(2)}, u32[]{:S(2)}) collective-permute-start(bf16[288,512]{1,0:T(8,128)(2,1)S(1)} %pack.1.refs_0_), channel_id=1, source_target_pairs={{0,14},{2,0},{4,2},{6,4},{8,6},{10,8},{12,10},{14,12},{1,15},{3,1}... | collective-permute-start | bytes 884744 | tf_op jit(solution)/shard_map/ppermute | solution.py:33
  35.7 9.5 %collective-permute-start.1 = (bf16[288,512]{1,0:T(8,128)(2,1)S(1)}, bf16[288,512]{1,0:T(8,128)(2,1)S(1)}, u32[]{:S(2)}, u32[]{:S(2)}) collective-permute-start(bf16[288,512]{1,0:T(8,128)(2,1)S(1)} %collective-permute-done.refs_1_), channel_id=1, source_target_pairs={{0,2},{2,4},{4,6},{6,8},{8,10},{10,12},{12,14},{14,0},{1,3},{3,5},... | collective-permute-start | bytes 884744 | tf_op jit(solution)/shard_map/ppermute | solution.py:33
  41.0 9.5 %collective-permute-start.4 = (bf16[288,512]{1,0:T(8,128)(2,1)S(1)}, bf16[288,512]{1,0:T(8,128)(2,1)S(1)}, u32[]{:S(2)}, u32[]{:S(2)}) collective-permute-start(bf16[288,512]{1,0:T(8,128)(2,1)S(1)} %collective-permute-done.3.refs_6_), channel_id=1, source_target_pairs={{0,14},{2,0},{4,2},{6,4},{8,6},{10,8},{12,10},{14,12},{1,15},{3,1}... | collective-permute-start | bytes 884744 | tf_op jit(solution)/shard_map/ppermute | solution.py:33
  45.2 9.0 %collective-permute-start.2 = (bf16[288,512]{1,0:T(8,128)(2,1)S(1)}, bf16[288,512]{1,0:T(8,128)(2,1)}, u32[]{:S(2)}, u32[]{:S(2)}) collective-permute-start(bf16[288,512]{1,0:T(8,128)(2,1)S(1)} %collective-permute-done.1.refs_2_), channel_id=1, source_target_pairs={{0,2},{2,4},{4,6},{6,8},{8,10},{10,12},{12,14},{14,0},{1,3},{3,5},... | collective-permute-start | bytes 884744 | tf_op jit(solution)/shard_map/ppermute | solution.py:33
  50.5 8.7 %collective-permute-start.5 = (bf16[288,512]{1,0:T(8,128)(2,1)S(1)}, bf16[288,512]{1,0:T(8,128)(2,1)S(1)}, u32[]{:S(2)}, u32[]{:S(2)}) collective-permute-start(bf16[288,512]{1,0:T(8,128)(2,1)S(1)} %collective-permute-done.4.refs_5_), channel_id=1, source_target_pairs={{0,14},{2,0},{4,2},{6,4},{8,6},{10,8},{12,10},{14,12},{1,15},{3,1}... | collective-permute-start | bytes 884744 | tf_op jit(solution)/shard_map/ppermute | solution.py:33
  61.6 30.7 %copy-start.10 = (s32[4]{0:T(128)S(1)}, s32[4]{0:T(128)}, u32[]{:S(2)}) copy-start(s32[4]{0:T(128)} %param.15) | copy-start | bytes 52
  61.6 36.9 %copy-start.1 = (bf16[256,2304]{1,0:T(8,128)(2,1)S(1)}, bf16[256,2304]{1,0:T(8,128)(2,1)}, u32[]{:S(2)}) copy-start(bf16[256,2304]{1,0:T(8,128)(2,1)} %tokens_ref.3) | copy-start | bytes 3538948
  61.6 36.9 %collective-permute-start.10 = (bf16[7,288,512]{2,1,0:T(8,128)(2,1)}, bf16[7,288,512]{2,1,0:T(8,128)(2,1)}, u32[]{:S(2)}, u32[]{:S(2)}) collective-permute-start(bf16[7,288,512]{2,1,0:T(8,128)(2,1)} %stack_up.1.early_ref), channel_id=1, source_target_pairs={{0,1},{1,0},{2,3},{3,2},{4,5},{5,4},{6,7},{7,6},{8,9},{9,8},{10,11... | collective-permute-start | bytes 6193160 | tf_op jit(solution)/shard_map/ppermute | solution.py:28
  69.2 13.4 %collective-permute-start.8 = (bf16[4,18,1024]{2,0,1:T(4,128)(2,1)}, bf16[4,18,1024]{2,0,1:T(4,128)(2,1)S(1)}, u32[]{:S(2)}, u32[]{:S(2)}) collective-permute-start(bf16[4,18,1024]{2,0,1:T(4,128)(2,1)} %bitcast.2), channel_id=1, source_target_pairs={{0,128},{128,0},{256,384},{384,256},{1,129},{129,1},{257,385},{385... | collective-permute-start | bytes 442376 | tf_op jit(solution)/shard_map/ppermute | solution.py:37
  75.0 12.0 %collective-permute-start.9 = (bf16[288,512]{1,0:T(8,128)(2,1)}, bf16[288,512]{1,0:T(8,128)(2,1)S(1)}, u32[]{:S(2)}, u32[]{:S(2)}) collective-permute-start(bf16[288,512]{1,0:T(8,128)(2,1)} %collective-permute-done.2.refs_3_), channel_id=1, source_target_pairs={{0,2},{2,4},{4,6},{6,8},{8,10},{10,12},{12,14},{14,0},{1,3},{3,5},... | collective-permute-start | bytes 884744 | tf_op jit(solution)/shard_map/ppermute | solution.py:33
  76.9 30.2 %all-to-all-start.2 = ((bf16[16,18,512]{2,1,0:T(8,128)(2,1)}), bf16[16,18,512]{2,1,0:T(8,128)(2,1)S(1)}, u32[]{:S(2)}, u32[]{:S(2)}) async-start(bf16[16,18,512]{2,1,0:T(8,128)(2,1)} %plane_total.1), calls=%async_computation.2 | async-start | bytes 786432 | tf_op jit(solution)/shard_map/all_to_all | solution.py:41
  87.0 11.5 %collective-permute-start.11 = (bf16[288,512]{1,0:T(8,128)(2,1)S(1)}, bf16[288,512]{1,0:T(8,128)(2,1)S(1)}, u32[]{:S(2)}, u32[]{:S(2)}) collective-permute-start(bf16[288,512]{1,0:T(8,128)(2,1)S(1)} %collective-permute-done.9.late_ref), channel_id=1, source_target_pairs={{0,1},{1,0},{2,3},{3,2},{4,5},{5,4},{6,7},{7,6},{8,9},{9,8},{10,11... | collective-permute-start | bytes 884744 | tf_op jit(solution)/shard_map/ppermute | solution.py:28
  92.3 14.8 %copy-start.7 = (bf16[1,18]{1,0:T(2,128)(2,1)S(1)}, bf16[1,18]{1,0:T(2,128)(2,1)}, u32[]{:S(2)}) copy-start(bf16[1,18]{1,0:T(2,128)(2,1)} %gain_ref.3) | copy-start | bytes 112
  92.4 14.8 %collective-permute-start.12 = (bf16[4,18,1024]{2,0,1:T(4,128)(2,1)S(1)}, bf16[4,18,1024]{2,0,1:T(4,128)(2,1)S(1)}, u32[]{:S(2)}, u32[]{:S(2)}) collective-permute-start(bf16[4,18,1024]{2,0,1:T(4,128)(2,1)S(1)} %add_convert_fusion), channel_id=1, source_target_pairs={{0,384},{128,256},{256,128},{384,0},{1,385},{129,257},{257,129},{3... | collective-permute-start | bytes 442376 | tf_op jit(solution)/shard_map/ppermute | solution.py:37
  98.5 1.0 copy-start.3
  99.6 7.6 %copy-start.5 = (bf16[1,18,1024]{2,1,0:T(8,128)(2,1)S(1)}, bf16[1,18,1024]{2,1,0:T(8,128)(2,1)}, u32[]{:S(2)}) copy-start(bf16[1,18,1024]{2,1,0:T(8,128)(2,1)} %weight_ref.3) | copy-start | bytes 110596
  99.6 8.4 %copy-start.8 = (f32[4,18,1024]{2,0,1:T(4,128)S(1)}, f32[4,18,1024]{2,0,1:T(4,128)}, u32[]{:S(2)}) copy-start(f32[4,18,1024]{2,0,1:T(4,128)} %param.14) | copy-start | bytes 884740
  99.6 8.4 %copy-start.9 = (f32[4,18,1024]{2,0,1:T(4,128)S(1)}, f32[4,18,1024]{2,0,1:T(4,128)}, u32[]{:S(2)}) copy-start(f32[4,18,1024]{2,0,1:T(4,128)} %param.13) | copy-start | bytes 884740

commit v4 on v3

--- a/solution.py
+++ b/solution.py
@@ -158,10 +158,10 @@
 def partial_product(core, tokens, others, cotangent, others_cot):
     rows, width = tokens.shape
     out = cotangent.shape[1]
-    step = width // 6
+    step = width // 3
     return pl.pallas_call(
         partial_kernel,
-        grid=(6,),
+        grid=(3,),
         out_shape=jax.ShapeDtypeStruct((width, out // 2), bf16),
         in_specs=[
             pl.BlockSpec(memory_space=pltpu.SMEM),
@@ -346,11 +346,11 @@
 
     delta, plane_sum = after((outer_delta[0], plane_sum))
     pair = (delta.astype(f32) + partner(delta, (1, 0, 3, 2)).astype(f32)).astype(bf16)
-    pair, late = after((pair, late))
     other_pair = partner(pair, (3, 2, 1, 0))
 
+    late_other, blocks = after((swap(late), blocks))
     layer_out, input_grad = project(
-        place, tokens, cotangent, early, late, early_other, swap(late)
+        place, tokens, cotangent, early, late, early_other, late_other
     )
 
     layer_out, other_pair, blocks = after((layer_out, other_pair, blocks))

time: 110 us -> 109 us (level)
  the two profiles are of different devices: /device:TPU:25 before, /device:TPU:72 now
where the time goes in v4:
time: 109 us; the launch traced here: 108 us
  starting transfers between devices  65.9 us (60%)
  waiting for transfers between devices  18.7 us (17%)
  Pallas kernels  14.2 us (13%)
  local copies, waits for them, and re-layouts  6.23 us (6%)
  other arithmetic  2.24 us (2%)
    ppermute x7, starting transfers between devices, turn(): lax.ppermute(values, 'y', [(i, (i + by) % count) for i in range(count)])  25.6 us
    all_to_all x3, starting transfers between devices, exchange(): return lax.all_to_all(values, axes, split_axis=0, concat_axis=0, tiled=True)  17.2 us
    ppermute x2, starting transfers between devices, partner(): return lax.ppermute(values, 'rep', list(enumerate(partners)))  14.8 us
    ppermute x7, waiting for transfers between devices, turn(): lax.ppermute(values, 'y', [(i, (i + by) % count) for i in range(count)])  11.9 us
    ppermute x4, starting transfers between devices, swap(): return lax.ppermute(values, 'core', [(0, 1), (1, 0)])  8.28 us
    pallas_call x1, Pallas kernels, project(): pl.pallas_call(project_kernel, grid=(2,), out_shape=(jax.ShapeDtypeStruct...  7.58 us
    unnamed x26, local copies, waits for them, and re-layouts  6.23 us
    ppermute x2, waiting for transfers between devices, partner(): return lax.ppermute(values, 'rep', list(enumerate(partners)))  4.83 us
  transfers between devices with their start and end apart: 16, of which 6 were waited for; matrix products, arithmetic and copies ran while one was open for 1% of the time, Pallas kernels for 12%

profile of v4, /device:TPU:72, one launch (start us, length us, event | category | flops | bytes accessed | tf_op | source)
XLA Modules:
  0.0 108.2 jit_solution(5499842662737320070)
XLA Ops:
  0.6 0.0 copy-start.6
  0.6 0.8 copy-done.6
  1.4 0.0 copy-start.8
  1.4 0.7 copy-done.8
  2.1 0.9 weigh.1
  2.9 1.9 %collective-permute-start.6 = (bf16[256,2304]{1,0:T(8,128)(2,1)}, bf16[256,2304]{1,0:T(8,128)(2,1)S(1)}, u32[]{:S(2)}, u32[]{:S(2)}) collective-permute-start(bf16[256,2304]{1,0:T(8,128)(2,1)} %tokens_ref.3), channel_id=1, source_target_pairs={{0,1},{1,0},{2,3},{3,2},{4,5},{5,4},{6,7},{7,6},{8,9},{9,8},{10,11... | collective-permute-start | bytes 3538952 | tf_op jit(solution)/shard_map/ppermute | solution.py:28
  4.9 2.4 %collective-permute-start.7 = (bf16[256,1024]{1,0:T(8,128)(2,1)}, bf16[256,1024]{1,0:T(8,128)(2,1)S(1)}, u32[]{:S(2)}, u32[]{:S(2)}) collective-permute-start(bf16[256,1024]{1,0:T(8,128)(2,1)} %cot_ref.3), channel_id=1, source_target_pairs={{0,1},{1,0},{2,3},{3,2},{4,5},{5,4},{6,7},{7,6},{8,9},{9,8},{10,11... | collective-permute-start | bytes 1572872 | tf_op jit(solution)/shard_map/ppermute | solution.py:28
  7.3 5.8 %all-to-all-start = ((bf16[16,18,512]{2,1,0:T(8,128)(2,1)}), bf16[16,18,512]{2,1,0:T(8,128)(2,1)S(1)}, u32[]{:S(2)}, u32[]{:S(2)}) async-start(bf16[16,18,512]{2,1,0:T(8,128)(2,1)} %weigh.1), calls=%async_computation | async-start | bytes 786432 | tf_op jit(solution)/shard_map/all_to_all | solution.py:41
  13.1 0.0 collective-permute-done.7.others_cot_ref
  13.1 0.0 collective-permute-done.6.others_ref
  13.1 0.0 copy-start.1
  13.1 1.3 %copy-done.1 = bf16[256,2304]{1,0:T(8,128)(2,1)S(1)} copy-done((bf16[256,2304]{1,0:T(8,128)(2,1)S(1)}, bf16[256,2304]{1,0:T(8,128)(2,1)}, u32[]{:S(2)}) %copy-start.1) | copy-done | bytes 1179672
  14.4 0.0 copy-start.3
  14.4 1.0 copy-done.3
  15.4 2.4 %partial.1 = bf16[2304,512]{1,0:T(8,128)(2,1)S(1)} custom-call(s32[1]{0:T(128)} %bitcast.1.core_ref, bf16[256,2304]{1,0:T(8,128)(2,1)S(1)} %copy-done.1, bf16[256,2304]{1,0:T(8,128)(2,1)S(1)} %collective-permute-done.6.others_ref, bf16[256,1024]{1,0:T(8,128)(2,1)S(1)} %copy-done.3, bf16[256,1024]{1,0:T(8,128)(2,1)S(1)} %collective-permute-done.7.others_cot_ref), custom_call_target="tpu_custom_call" | custom-call | flops 1207959552 | bytes 3538944 | tf_op jit(solution)/shard_map/partial/pallas_call | solution.py:162
  17.8 0.0 copy-start
  17.8 1.4 %copy-done = bf16[2304,512]{1,0:T(8,128)(2,1)} copy-done((bf16[2304,512]{1,0:T(8,128)(2,1)}, bf16[2304,512]{1,0:T(8,128)(2,1)S(1)}, u32[]{:S(2)}) %copy-start) | copy-done | bytes 2359320
  19.2 1.9 %all-to-all-done.parts_ref = bf16[16,18,512]{2,1,0:T(8,128)(2,1)S(1)} async-done(((bf16[16,18,512]{2,1,0:T(8,128)(2,1)}), bf16[16,18,512]{2,1,0:T(8,128)(2,1)S(1)}, u32[]{:S(2)}, u32[]{:S(2)}) %all-to-all-start) | async-done | bytes 294944 | tf_op jit(solution)/shard_map/all_to_all | solution.py:41
  21.2 5.0 %all-to-all-start.1 = ((bf16[8,288,512]{2,1,0:T(8,128)(2,1)}), bf16[8,288,512]{2,1,0:T(8,128)(2,1)S(1)}, u32[]{:S(2)}, u32[]{:S(2)}) async-start(bf16[8,288,512]{2,1,0:T(8,128)(2,1)} %bitcast.5), calls=%async_computation.1 | async-start | bytes 4718592 | tf_op jit(solution)/shard_map/all_to_all | solution.py:41
  26.2 3.5 %collective-permute-start = (bf16[288,512]{1,0:T(8,128)(2,1)S(1)}, bf16[288,512]{1,0:T(8,128)(2,1)S(1)}, u32[]{:S(2)}, u32[]{:S(2)}) collective-permute-start(bf16[288,512]{1,0:T(8,128)(2,1)S(1)} %pack.1.refs_0_), channel_id=1, source_target_pairs={{0,2},{2,4},{4,6},{6,8},{8,10},{10,12},{12,14},{14,0},{1,3},{3,5},... | collective-permute-start | bytes 884744 | tf_op jit(solution)/shard_map/ppermute | solution.py:33
  29.7 3.5 %collective-permute-start.3 = (bf16[288,512]{1,0:T(8,128)(2,1)S(1)}, bf16[288,512]{1,0:T(8,128)(2,1)S(1)}, u32[]{:S(2)}, u32[]{:S(2)}) collective-permute-start(bf16[288,512]{1,0:T(8,128)(2,1)S(1)} %pack.1.refs_0_), channel_id=1, source_target_pairs={{0,14},{2,0},{4,2},{6,4},{8,6},{10,8},{12,10},{14,12},{1,15},{3,1}... | collective-permute-start | bytes 884744 | tf_op jit(solution)/shard_map/ppermute | solution.py:33
  33.2 4.3 %collective-permute-done.refs_1_ = bf16[288,512]{1,0:T(8,128)(2,1)S(1)} collective-permute-done((bf16[288,512]{1,0:T(8,128)(2,1)S(1)}, bf16[288,512]{1,0:T(8,128)(2,1)S(1)}, u32[]{:S(2)}, u32[]{:S(2)}) %collective-permute-start) | collective-permute-done | bytes 294944 | tf_op jit(solution)/shard_map/ppermute | solution.py:33
  37.5 2.1 %collective-permute-start.1 = (bf16[288,512]{1,0:T(8,128)(2,1)S(1)}, bf16[288,512]{1,0:T(8,128)(2,1)S(1)}, u32[]{:S(2)}, u32[]{:S(2)}) collective-permute-start(bf16[288,512]{1,0:T(8,128)(2,1)S(1)} %collective-permute-done.refs_1_), channel_id=1, source_target_pairs={{0,2},{2,4},{4,6},{6,8},{8,10},{10,12},{12,14},{14,0},{1,3},{3,5},... | collective-permute-start | bytes 884744 | tf_op jit(solution)/shard_map/ppermute | solution.py:33
  39.6 0.0 collective-permute-done.3.refs_6_
  39.6 4.7 %collective-permute-start.4 = (bf16[288,512]{1,0:T(8,128)(2,1)S(1)}, bf16[288,512]{1,0:T(8,128)(2,1)S(1)}, u32[]{:S(2)}, u32[]{:S(2)}) collective-permute-start(bf16[288,512]{1,0:T(8,128)(2,1)S(1)} %collective-permute-done.3.refs_6_), channel_id=1, source_target_pairs={{0,14},{2,0},{4,2},{6,4},{8,6},{10,8},{12,10},{14,12},{1,15},{3,1}... | collective-permute-start | bytes 884744 | tf_op jit(solution)/shard_map/ppermute | solution.py:33
  44.3 3.4 %collective-permute-done.1.refs_2_ = bf16[288,512]{1,0:T(8,128)(2,1)S(1)} collective-permute-done((bf16[288,512]{1,0:T(8,128)(2,1)S(1)}, bf16[288,512]{1,0:T(8,128)(2,1)S(1)}, u32[]{:S(2)}, u32[]{:S(2)}) %collective-permute-start.1) | collective-permute-done | bytes 294944 | tf_op jit(solution)/shard_map/ppermute | solution.py:33
  47.6 1.9 %collective-permute-start.2 = (bf16[288,512]{1,0:T(8,128)(2,1)S(1)}, bf16[288,512]{1,0:T(8,128)(2,1)S(1)}, u32[]{:S(2)}, u32[]{:S(2)}) collective-permute-start(bf16[288,512]{1,0:T(8,128)(2,1)S(1)} %collective-permute-done.1.refs_2_), channel_id=1, source_target_pairs={{0,2},{2,4},{4,6},{6,8},{8,10},{10,12},{12,14},{14,0},{1,3},{3,5},... | collective-permute-start | bytes 884744 | tf_op jit(solution)/shard_map/ppermute | solution.py:33
  49.5 0.0 collective-permute-done.4.refs_5_
  49.5 4.9 %collective-permute-start.5 = (bf16[288,512]{1,0:T(8,128)(2,1)S(1)}, bf16[288,512]{1,0:T(8,128)(2,1)S(1)}, u32[]{:S(2)}, u32[]{:S(2)}) collective-permute-start(bf16[288,512]{1,0:T(8,128)(2,1)S(1)} %collective-permute-done.4.refs_5_), channel_id=1, source_target_pairs={{0,14},{2,0},{4,2},{6,4},{8,6},{10,8},{12,10},{14,12},{1,15},{3,1}... | collective-permute-start | bytes 884744 | tf_op jit(solution)/shard_map/ppermute | solution.py:33
  54.4 2.7 %collective-permute-done.2.refs_3_ = bf16[288,512]{1,0:T(8,128)(2,1)S(1)} collective-permute-done((bf16[288,512]{1,0:T(8,128)(2,1)S(1)}, bf16[288,512]{1,0:T(8,128)(2,1)S(1)}, u32[]{:S(2)}, u32[]{:S(2)}) %collective-permute-start.2) | collective-permute-done | bytes 294944 | tf_op jit(solution)/shard_map/ppermute | solution.py:33
  57.2 0.0 copy-start.5
  57.2 1.5 %collective-permute-done.5.refs_4_ = bf16[288,512]{1,0:T(8,128)(2,1)S(1)} collective-permute-done((bf16[288,512]{1,0:T(8,128)(2,1)S(1)}, bf16[288,512]{1,0:T(8,128)(2,1)S(1)}, u32[]{:S(2)}, u32[]{:S(2)}) %collective-permute-start.5) | collective-permute-done | bytes 294944 | tf_op jit(solution)/shard_map/ppermute | solution.py:33
  58.7 1.5 %stack_up.1.early_ref = bf16[7,288,512]{2,1,0:T(8,128)(2,1)} custom-call(bf16[288,512]{1,0:T(8,128)(2,1)S(1)} %pack.1.refs_0_, bf16[288,512]{1,0:T(8,128)(2,1)S(1)} %collective-permute-done.refs_1_, bf16[288,512]{1,0:T(8,128)(2,1)S(1)} %collective-permute-done.1.refs_2_, bf16[288,512]{1,0:T(8,128)(2,1)S(1)} %collective-permute-done.2.refs_3_, ...), custom_call_target="tpu_custom_call" | custom-call | bytes 4128768 | tf_op jit(solution)/shard_map/stack_up/pallas_call | solution.py:103
  60.1 0.0 copy-done.5
  60.1 0.0 copy-start.12
  60.1 0.0 copy-start.2
  60.1 2.0 %collective-permute-start.9 = (bf16[7,288,512]{2,1,0:T(8,128)(2,1)}, bf16[7,288,512]{2,1,0:T(8,128)(2,1)}, u32[]{:S(2)}, u32[]{:S(2)}) collective-permute-start(bf16[7,288,512]{2,1,0:T(8,128)(2,1)} %stack_up.1.early_ref), channel_id=1, source_target_pairs={{0,1},{1,0},{2,3},{3,2},{4,5},{5,4},{6,7},{7,6},{8,9},{9,8},{10,11... | collective-permute-start | bytes 6193160 | tf_op jit(solution)/shard_map/ppermute | solution.py:28
  62.2 0.0 all-to-all-done.1.parts_ref
  62.2 5.1 %collective-permute-start.8 = (bf16[288,512]{1,0:T(8,128)(2,1)}, bf16[288,512]{1,0:T(8,128)(2,1)}, u32[]{:S(2)}, u32[]{:S(2)}) collective-permute-start(bf16[288,512]{1,0:T(8,128)(2,1)} %copy-done.5), channel_id=1, source_target_pairs={{0,2},{2,4},{4,6},{6,8},{8,10},{10,12},{12,14},{14,0},{1,3},{3,5},... | collective-permute-start | bytes 884744 | tf_op jit(solution)/shard_map/ppermute | solution.py:33
  67.3 1.1 plane_total.1
  68.4 6.4 %all-to-all-start.2 = ((bf16[16,18,512]{2,1,0:T(8,128)(2,1)}), bf16[16,18,512]{2,1,0:T(8,128)(2,1)S(1)}, u32[]{:S(2)}, u32[]{:S(2)}) async-start(bf16[16,18,512]{2,1,0:T(8,128)(2,1)} %plane_total.1), calls=%async_computation.2 | async-start | bytes 786432 | tf_op jit(solution)/shard_map/all_to_all | solution.py:41
  74.8 5.7 %collective-permute-start.11 = (bf16[4,18,1024]{2,0,1:T(4,128)(2,1)}, bf16[4,18,1024]{2,0,1:T(4,128)(2,1)S(1)}, u32[]{:S(2)}, u32[]{:S(2)}) collective-permute-start(bf16[4,18,1024]{2,0,1:T(4,128)(2,1)} %bitcast.6), channel_id=1, source_target_pairs={{0,128},{128,0},{256,384},{384,256},{1,129},{129,1},{257,385},{385... | collective-permute-start | bytes 442376 | tf_op jit(solution)/shard_map/ppermute | solution.py:37
  80.5 0.0 copy-done.12
  80.5 0.0 collective-permute-done.8.late_ref
  80.5 1.9 %collective-permute-start.10 = (bf16[288,512]{1,0:T(8,128)(2,1)}, bf16[288,512]{1,0:T(8,128)(2,1)S(1)}, u32[]{:S(2)}, u32[]{:S(2)}) collective-permute-start(bf16[288,512]{1,0:T(8,128)(2,1)} %collective-permute-done.8.late_ref), channel_id=1, source_target_pairs={{0,1},{1,0},{2,3},{3,2},{4,5},{5,4},{6,7},{7,6},{8,9},{9,8},{10,11... | collective-permute-start | bytes 884744 | tf_op jit(solution)/shard_map/ppermute | solution.py:28
  82.4 0.1 pad_add_fusion.place_ref
  82.5 4.8 %collective-permute-done.11 = bf16[4,18,1024]{2,0,1:T(4,128)(2,1)S(1)} collective-permute-done((bf16[4,18,1024]{2,0,1:T(4,128)(2,1)}, bf16[4,18,1024]{2,0,1:T(4,128)(2,1)S(1)}, u32[]{:S(2)}, u32[]{:S(2)}) %collective-permute-start.11) | collective-permute-done | bytes 147488 | tf_op jit(solution)/shard_map/ppermute | solution.py:37
  87.4 0.0 copy-start.7
  87.4 1.0 add_convert_fusion
  88.4 9.1 %collective-permute-start.12 = (bf16[4,18,1024]{2,0,1:T(4,128)(2,1)S(1)}, bf16[4,18,1024]{2,0,1:T(4,128)(2,1)S(1)}, u32[]{:S(2)}, u32[]{:S(2)}) collective-permute-start(bf16[4,18,1024]{2,0,1:T(4,128)(2,1)S(1)} %add_convert_fusion), channel_id=1, source_target_pairs={{0,384},{128,256},{256,128},{384,0},{1,385},{129,257},{257,129},{3... | collective-permute-start | bytes 442376 | tf_op jit(solution)/shard_map/ppermute | solution.py:37
  97.5 0.0 all-to-all-done.2.blocks_ref
  97.5 0.0 collective-permute-done.10.late_other_ref
  97.6 0.0 collective-permute-done.9.early_other_ref
  97.6 0.0 copy-done.2
  97.6 0.0 copy-start.4
  97.6 1.0 copy-done.4
  98.6 7.6 %project.1 = (bf16[256,1024]{1,0:T(8,128)(2,1)}, bf16[256,2304]{1,0:T(8,128)(2,1)}) custom-call(s32[2]{0:T(128)S(1)} %pad_add_fusion.place_ref, bf16[256,2304]{1,0:T(8,128)(2,1)S(1)} %copy-done.2, bf16[256,1024]{1,0:T(8,128)(2,1)S(1)} %copy-done.4, bf16[7,288,512]{2,1,0:T(8,128)(2,1)} %stack_up.1.early_ref, ...), custom_call_target="tpu_custom_call" | custom-call | flops 2415919104 | bytes 8126464 | tf_op jit(solution)/shard_map/project/pallas_call | solution.py:286
  106.2 0.0 collective-permute-done.12
  106.2 0.0 copy-done.7
  106.2 0.0 copy-done.9
  106.2 0.8 owner_total.1
  107.0 0.0 copy-done.10
  107.0 0.0 copy-done.11
  107.0 1.1 %fusion = (f32[4,18,1024]{2,0,1:T(4,128)}, f32[4,18,1024]{2,0,1:T(4,128)}) fusion(f32[4,18,1024]{2,0,1:T(4,128)S(1)} %copy-done.10, bf16[4,18,1024]{2,0,1:T(4,128)(2,1)S(1)} %collective-permute-done.12, bf16[4,18,1024]{2,0,1:T(4,128)(2,1)S(1)} %add_convert_fusion, pred[4]{0:T(512)(128)(4,1)S(1)} %broadcast_compare_fusion, f32[4,18,1024]{2,0,1:T(4,128)S(1)} %copy-done.11), kind=kLoop, calls=%fused_computation.2 | loop fusion | flops 884736 | bytes 1474564 | tf_op jit(solution)/shard_map/jit(_where)/select_n | solution.py:22
  (5 shorter events, 0.1 us)
Async XLA Ops:
  0.6 0.8 copy-start.6
  1.4 0.7 copy-start.8
  2.9 10.1 %collective-permute-start.6 = (bf16[256,2304]{1,0:T(8,128)(2,1)}, bf16[256,2304]{1,0:T(8,128)(2,1)S(1)}, u32[]{:S(2)}, u32[]{:S(2)}) collective-permute-start(bf16[256,2304]{1,0:T(8,128)(2,1)} %tokens_ref.3), channel_id=1, source_target_pairs={{0,1},{1,0},{2,3},{3,2},{4,5},{5,4},{6,7},{7,6},{8,9},{9,8},{10,11... | collective-permute-start | bytes 3538952 | tf_op jit(solution)/shard_map/ppermute | solution.py:28
  4.9 8.2 %collective-permute-start.7 = (bf16[256,1024]{1,0:T(8,128)(2,1)}, bf16[256,1024]{1,0:T(8,128)(2,1)S(1)}, u32[]{:S(2)}, u32[]{:S(2)}) collective-permute-start(bf16[256,1024]{1,0:T(8,128)(2,1)} %cot_ref.3), channel_id=1, source_target_pairs={{0,1},{1,0},{2,3},{3,2},{4,5},{5,4},{6,7},{7,6},{8,9},{9,8},{10,11... | collective-permute-start | bytes 1572872 | tf_op jit(solution)/shard_map/ppermute | solution.py:28
  7.3 13.9 %all-to-all-start = ((bf16[16,18,512]{2,1,0:T(8,128)(2,1)}), bf16[16,18,512]{2,1,0:T(8,128)(2,1)S(1)}, u32[]{:S(2)}, u32[]{:S(2)}) async-start(bf16[16,18,512]{2,1,0:T(8,128)(2,1)} %weigh.1), calls=%async_computation | async-start | bytes 786432 | tf_op jit(solution)/shard_map/all_to_all | solution.py:41
  13.1 1.3 %copy-start.1 = (bf16[256,2304]{1,0:T(8,128)(2,1)S(1)}, bf16[256,2304]{1,0:T(8,128)(2,1)}, u32[]{:S(2)}) copy-start(bf16[256,2304]{1,0:T(8,128)(2,1)} %tokens_ref.3) | copy-start | bytes 3538948
  14.4 1.0 copy-start.3
  17.8 1.4 %copy-start = (bf16[2304,512]{1,0:T(8,128)(2,1)}, bf16[2304,512]{1,0:T(8,128)(2,1)S(1)}, u32[]{:S(2)}) copy-start(bf16[2304,512]{1,0:T(8,128)(2,1)S(1)} %partial.1) | copy-start | bytes 7077892
  21.2 41.0 %all-to-all-start.1 = ((bf16[8,288,512]{2,1,0:T(8,128)(2,1)}), bf16[8,288,512]{2,1,0:T(8,128)(2,1)S(1)}, u32[]{:S(2)}, u32[]{:S(2)}) async-start(bf16[8,288,512]{2,1,0:T(8,128)(2,1)} %bitcast.5), calls=%async_computation.1 | async-start | bytes 4718592 | tf_op jit(solution)/shard_map/all_to_all | solution.py:41
  26.2 11.3 %collective-permute-start = (bf16[288,512]{1,0:T(8,128)(2,1)S(1)}, bf16[288,512]{1,0:T(8,128)(2,1)S(1)}, u32[]{:S(2)}, u32[]{:S(2)}) collective-permute-start(bf16[288,512]{1,0:T(8,128)(2,1)S(1)} %pack.1.refs_0_), channel_id=1, source_target_pairs={{0,2},{2,4},{4,6},{6,8},{8,10},{10,12},{12,14},{14,0},{1,3},{3,5},... | collective-permute-start | bytes 884744 | tf_op jit(solution)/shard_map/ppermute | solution.py:33
  29.7 9.9 %collective-permute-start.3 = (bf16[288,512]{1,0:T(8,128)(2,1)S(1)}, bf16[288,512]{1,0:T(8,128)(2,1)S(1)}, u32[]{:S(2)}, u32[]{:S(2)}) collective-permute-start(bf16[288,512]{1,0:T(8,128)(2,1)S(1)} %pack.1.refs_0_), channel_id=1, source_target_pairs={{0,14},{2,0},{4,2},{6,4},{8,6},{10,8},{12,10},{14,12},{1,15},{3,1}... | collective-permute-start | bytes 884744 | tf_op jit(solution)/shard_map/ppermute | solution.py:33
  37.5 10.1 %collective-permute-start.1 = (bf16[288,512]{1,0:T(8,128)(2,1)S(1)}, bf16[288,512]{1,0:T(8,128)(2,1)S(1)}, u32[]{:S(2)}, u32[]{:S(2)}) collective-permute-start(bf16[288,512]{1,0:T(8,128)(2,1)S(1)} %collective-permute-done.refs_1_), channel_id=1, source_target_pairs={{0,2},{2,4},{4,6},{6,8},{8,10},{10,12},{12,14},{14,0},{1,3},{3,5},... | collective-permute-start | bytes 884744 | tf_op jit(solution)/shard_map/ppermute | solution.py:33
  39.6 10.0 %collective-permute-start.4 = (bf16[288,512]{1,0:T(8,128)(2,1)S(1)}, bf16[288,512]{1,0:T(8,128)(2,1)S(1)}, u32[]{:S(2)}, u32[]{:S(2)}) collective-permute-start(bf16[288,512]{1,0:T(8,128)(2,1)S(1)} %collective-permute-done.3.refs_6_), channel_id=1, source_target_pairs={{0,14},{2,0},{4,2},{6,4},{8,6},{10,8},{12,10},{14,12},{1,15},{3,1}... | collective-permute-start | bytes 884744 | tf_op jit(solution)/shard_map/ppermute | solution.py:33
  47.6 9.5 %collective-permute-start.2 = (bf16[288,512]{1,0:T(8,128)(2,1)S(1)}, bf16[288,512]{1,0:T(8,128)(2,1)S(1)}, u32[]{:S(2)}, u32[]{:S(2)}) collective-permute-start(bf16[288,512]{1,0:T(8,128)(2,1)S(1)} %collective-permute-done.1.refs_2_), channel_id=1, source_target_pairs={{0,2},{2,4},{4,6},{6,8},{8,10},{10,12},{12,14},{14,0},{1,3},{3,5},... | collective-permute-start | bytes 884744 | tf_op jit(solution)/shard_map/ppermute | solution.py:33
  49.5 9.1 %collective-permute-start.5 = (bf16[288,512]{1,0:T(8,128)(2,1)S(1)}, bf16[288,512]{1,0:T(8,128)(2,1)S(1)}, u32[]{:S(2)}, u32[]{:S(2)}) collective-permute-start(bf16[288,512]{1,0:T(8,128)(2,1)S(1)} %collective-permute-done.4.refs_5_), channel_id=1, source_target_pairs={{0,14},{2,0},{4,2},{6,4},{8,6},{10,8},{12,10},{14,12},{1,15},{3,1}... | collective-permute-start | bytes 884744 | tf_op jit(solution)/shard_map/ppermute | solution.py:33
  57.2 3.0 %copy-start.5 = (bf16[288,512]{1,0:T(8,128)(2,1)}, bf16[288,512]{1,0:T(8,128)(2,1)S(1)}, u32[]{:S(2)}) copy-start(bf16[288,512]{1,0:T(8,128)(2,1)S(1)} %collective-permute-done.2.refs_3_) | copy-start | bytes 884740
  60.1 20.3 %copy-start.12 = (s32[4]{0:T(128)S(1)}, s32[4]{0:T(128)}, u32[]{:S(2)}) copy-start(s32[4]{0:T(128)} %param.15) | copy-start | bytes 52
  60.1 37.4 %copy-start.2 = (bf16[256,2304]{1,0:T(8,128)(2,1)S(1)}, bf16[256,2304]{1,0:T(8,128)(2,1)}, u32[]{:S(2)}) copy-start(bf16[256,2304]{1,0:T(8,128)(2,1)} %tokens_ref.3) | copy-start | bytes 3538948
  60.1 37.4 %collective-permute-start.9 = (bf16[7,288,512]{2,1,0:T(8,128)(2,1)}, bf16[7,288,512]{2,1,0:T(8,128)(2,1)}, u32[]{:S(2)}, u32[]{:S(2)}) collective-permute-start(bf16[7,288,512]{2,1,0:T(8,128)(2,1)} %stack_up.1.early_ref), channel_id=1, source_target_pairs={{0,1},{1,0},{2,3},{3,2},{4,5},{5,4},{6,7},{7,6},{8,9},{9,8},{10,11... | collective-permute-start | bytes 6193160 | tf_op jit(solution)/shard_map/ppermute | solution.py:28
  62.2 18.3 %collective-permute-start.8 = (bf16[288,512]{1,0:T(8,128)(2,1)}, bf16[288,512]{1,0:T(8,128)(2,1)}, u32[]{:S(2)}, u32[]{:S(2)}) collective-permute-start(bf16[288,512]{1,0:T(8,128)(2,1)} %copy-done.5), channel_id=1, source_target_pairs={{0,2},{2,4},{4,6},{6,8},{8,10},{10,12},{12,14},{14,0},{1,3},{3,5},... | collective-permute-start | bytes 884744 | tf_op jit(solution)/shard_map/ppermute | solution.py:33
  68.4 29.1 %all-to-all-start.2 = ((bf16[16,18,512]{2,1,0:T(8,128)(2,1)}), bf16[16,18,512]{2,1,0:T(8,128)(2,1)S(1)}, u32[]{:S(2)}, u32[]{:S(2)}) async-start(bf16[16,18,512]{2,1,0:T(8,128)(2,1)} %plane_total.1), calls=%async_computation.2 | async-start | bytes 786432 | tf_op jit(solution)/shard_map/all_to_all | solution.py:41
  74.8 12.5 %collective-permute-start.11 = (bf16[4,18,1024]{2,0,1:T(4,128)(2,1)}, bf16[4,18,1024]{2,0,1:T(4,128)(2,1)S(1)}, u32[]{:S(2)}, u32[]{:S(2)}) collective-permute-start(bf16[4,18,1024]{2,0,1:T(4,128)(2,1)} %bitcast.6), channel_id=1, source_target_pairs={{0,128},{128,0},{256,384},{384,256},{1,129},{129,1},{257,385},{385... | collective-permute-start | bytes 442376 | tf_op jit(solution)/shard_map/ppermute | solution.py:37
  80.5 17.0 %collective-permute-start.10 = (bf16[288,512]{1,0:T(8,128)(2,1)}, bf16[288,512]{1,0:T(8,128)(2,1)S(1)}, u32[]{:S(2)}, u32[]{:S(2)}) collective-permute-start(bf16[288,512]{1,0:T(8,128)(2,1)} %collective-permute-done.8.late_ref), channel_id=1, source_target_pairs={{0,1},{1,0},{2,3},{3,2},{4,5},{5,4},{6,7},{7,6},{8,9},{9,8},{10,11... | collective-permute-start | bytes 884744 | tf_op jit(solution)/shard_map/ppermute | solution.py:28
  87.4 18.9 %copy-start.7 = (bf16[1,18,1024]{2,1,0:T(8,128)(2,1)S(1)}, bf16[1,18,1024]{2,1,0:T(8,128)(2,1)}, u32[]{:S(2)}) copy-start(bf16[1,18,1024]{2,1,0:T(8,128)(2,1)} %weight_ref.3) | copy-start | bytes 110596
  87.4 18.9 %copy-start.9 = (bf16[1,18]{1,0:T(2,128)(2,1)S(1)}, bf16[1,18]{1,0:T(2,128)(2,1)}, u32[]{:S(2)}) copy-start(bf16[1,18]{1,0:T(2,128)(2,1)} %gain_ref.3) | copy-start | bytes 112
  87.4 19.7 %copy-start.10 = (f32[4,18,1024]{2,0,1:T(4,128)S(1)}, f32[4,18,1024]{2,0,1:T(4,128)}, u32[]{:S(2)}) copy-start(f32[4,18,1024]{2,0,1:T(4,128)} %param.14) | copy-start | bytes 884740
  88.4 17.8 %collective-permute-start.12 = (bf16[4,18,1024]{2,0,1:T(4,128)(2,1)S(1)}, bf16[4,18,1024]{2,0,1:T(4,128)(2,1)S(1)}, u32[]{:S(2)}, u32[]{:S(2)}) collective-permute-start(bf16[4,18,1024]{2,0,1:T(4,128)(2,1)S(1)} %add_convert_fusion), channel_id=1, source_target_pairs={{0,384},{128,256},{256,128},{384,0},{1,385},{129,257},{257,129},{3... | collective-permute-start | bytes 442376 | tf_op jit(solution)/shard_map/ppermute | solution.py:37
  97.6 1.0 copy-start.4
  98.6 8.4 %copy-start.11 = (f32[4,18,1024]{2,0,1:T(4,128)S(1)}, f32[4,18,1024]{2,0,1:T(4,128)}, u32[]{:S(2)}) copy-start(f32[4,18,1024]{2,0,1:T(4,128)} %param.13) | copy-start | bytes 884740
